TPU v7x, 32 devices: a whole 2x2x4 slice. The times are simulated.
32 devices in a mesh: section: 2 (over x), dp: 16 (over z, y, core).
Axes of the slice: x: 2, y: 2, z: 4, core: 2. Of those that a mesh axis runs over, the one named last changes fastest.
Arguments:
- clip_tokens: bfloat16 [2, 16, 6, 320, 512], P(None, 'dp'), may hold values from -6 to 6
- window_cols: int32 [2, 16], P(None, 'dp'), may hold values from 3 to 5, as said below
- time_groups: int32 [2, 16, 6], P(None, 'dp'), may hold values from 0 to 4, never falling along the last dimension, each value on 1 to 2 neighbouring positions
- cotangent: bfloat16 [2, 16, 6, 320, 512], P(None, 'dp'), may hold values from -6 to 6
- attention_gain: float32 [2, 512], P('section'), may hold values from 0.5 to 1.5
- attention_bias: float32 [2, 512], P('section'), may hold values from -2.5 to 2.5
- projection_in: bfloat16 [2, 512, 1536], P('section'), may hold values from -0.25 to 0.25
- projection_out: bfloat16 [2, 512, 512], P('section'), may hold values from -0.5 to 0.5
- output_bias: float32 [2, 512], P('section'), may hold values from -2.5 to 2.5
- feedforward_gain: float32 [2, 512], P('section'), may hold values from 0.5 to 1.5
- feedforward_bias: float32 [2, 512], P('section'), may hold values from -2.5 to 2.5
- up_weight: bfloat16 [2, 512, 2048], P('section'), may hold values from -0.25 to 0.25
- up_bias: float32 [2, 2048], P('section'), may hold values from -2.5 to 2.5
- down_weight: bfloat16 [2, 2048, 512], P('section'), may hold values from -0.125 to 0.125
- down_bias: float32 [2, 512], P('section'), may hold values from -2.5 to 2.5
Outputs:
- activations: bfloat16 [2, 2, 16, 6, 320, 512], P('section', None, 'dp')
- input_grads: bfloat16 [2, 2, 16, 6, 320, 512], P('section', None, 'dp')
- attention_gain_grad: float32 [2, 512], P('section')
- attention_bias_grad: float32 [2, 512], P('section')
- projection_in_grad: float32 [2, 512, 1536], P('section')
- projection_out_grad: float32 [2, 512, 512], P('section')
- output_bias_grad: float32 [2, 512], P('section')
- feedforward_gain_grad: float32 [2, 512], P('section')
- feedforward_bias_grad: float32 [2, 512], P('section')
- up_weight_grad: float32 [2, 512, 2048], P('section')
- up_bias_grad: float32 [2, 2048], P('section')
- down_weight_grad: float32 [2, 2048, 512], P('section')
- down_bias_grad: float32 [2, 512], P('section')
Inputs may be any that keep to these rules, and one draw needn't show every extreme that they name: `window_cols`: in every micro-batch some band has 5 windows. `time_groups`: time groups never fall along the frames; every group 0 to 4 holds a frame.
All inputs are finite; a program needn't handle non-finite values.
Results may differ from a plain program's by a relative error of at most 0.02.
Values may be sent and summed in bfloat16 or wider, within the bound.
A program may use at most 384 MiB of HBM per device.

v0:
```python
from functools import partial

import jax
import jax.numpy as jnp
from jax import lax
from jax.sharding import PartitionSpec as P

HEADS = 8
WCAP = 5


EPSILON = 1e-05
MASKED = -1e30


def shifted(value, axis, steps):
    count = lax.axis_size(axis)
    initial, last = (max(0, -steps), min(count, count - steps))
    return lax.ppermute(value, axis, [(source, source + steps) for source in range(initial, last)])


def normalize(values, gain, shift):
    center = jnp.mean(values, axis=-1, keepdims=True)
    centered = values - center
    spread = jnp.mean(centered * centered, axis=-1, keepdims=True)
    return centered * lax.rsqrt(spread + EPSILON) * gain + shift


def window_forward(query, keys, values, allowed, scale, window):
    count = query.shape[0] // window
    head_dim = query.shape[1] // HEADS
    q_win = query.reshape(count, window, HEADS, head_dim)
    k_win = keys.reshape(count, window, HEADS, head_dim)
    v_win = values.reshape(count, window, HEADS, head_dim)
    scores = jnp.einsum("gqhd,gkhd->ghqk", q_win, k_win, preferred_element_type=jnp.float32) * scale
    total = jax.nn.logsumexp(scores, axis=-1, keepdims=True)
    probs = jnp.exp(scores - total).astype(jnp.bfloat16)
    mixed = jnp.einsum("ghqk,gkhd->gqhd", probs, v_win, preferred_element_type=jnp.float32).astype(
        jnp.bfloat16
    )
    logsum = jnp.transpose(total[..., 0], (0, 2, 1)).reshape(query.shape[0], HEADS)
    return (mixed.reshape(query.shape[0], query.shape[1]), logsum)


def frame_forward(query, keys, values, allowed, scale, window):
    frames = allowed.shape[0]
    head_dim = query.shape[1] // HEADS
    q_frm = query.reshape(frames, -1, HEADS, head_dim)
    k_frm = keys.reshape(frames, -1, HEADS, head_dim)
    v_frm = values.reshape(frames, -1, HEADS, head_dim)
    scores = jnp.einsum("ibhd,jbhd->bhij", q_frm, k_frm, preferred_element_type=jnp.float32) * scale
    scores = jnp.where(allowed, scores, MASKED)
    total = jax.nn.logsumexp(scores, axis=-1, keepdims=True)
    probs = jnp.exp(scores - total).astype(jnp.bfloat16)
    mixed = jnp.einsum("bhij,jbhd->ibhd", probs, v_frm, preferred_element_type=jnp.float32).astype(
        jnp.bfloat16
    )
    logsum = jnp.transpose(total[..., 0], (2, 0, 1)).reshape(query.shape[0], HEADS)
    return (mixed.reshape(query.shape[0], query.shape[1]), logsum)


def window_backward(query, keys, values, logsum, upstream, allowed, scale, window):
    count = query.shape[0] // window
    head_dim = query.shape[1] // HEADS
    q_win = query.reshape(count, window, HEADS, head_dim)
    k_win = keys.reshape(count, window, HEADS, head_dim)
    v_win = values.reshape(count, window, HEADS, head_dim)
    up_win = upstream.reshape(count, window, HEADS, head_dim)
    total = jnp.transpose(logsum.reshape(count, window, HEADS), (0, 2, 1))[..., None]
    scores = jnp.einsum("gqhd,gkhd->ghqk", q_win, k_win, preferred_element_type=jnp.float32) * scale
    probs = jnp.exp(scores - total)
    value_grad = jnp.einsum(
        "ghqk,gqhd->gkhd", probs.astype(jnp.bfloat16), up_win, preferred_element_type=jnp.float32
    )
    prob_grad = jnp.einsum("gqhd,gkhd->ghqk", up_win, v_win, preferred_element_type=jnp.float32)
    score_grad = (probs * (prob_grad - jnp.sum(probs * prob_grad, axis=-1, keepdims=True))).astype(
        jnp.bfloat16
    )
    query_grad = (
        jnp.einsum("ghqk,gkhd->gqhd", score_grad, k_win, preferred_element_type=jnp.float32) * scale
    )
    key_grad = (
        jnp.einsum("ghqk,gqhd->gkhd", score_grad, q_win, preferred_element_type=jnp.float32) * scale
    )
    shape_two = (query.shape[0], query.shape[1])
    return jnp.concatenate(
        [query_grad.reshape(shape_two), key_grad.reshape(shape_two), value_grad.reshape(shape_two)],
        axis=1,
    )


def frame_backward(query, keys, values, logsum, upstream, allowed, scale, window):
    frames = allowed.shape[0]
    head_dim = query.shape[1] // HEADS
    q_frm = query.reshape(frames, -1, HEADS, head_dim)
    k_frm = keys.reshape(frames, -1, HEADS, head_dim)
    v_frm = values.reshape(frames, -1, HEADS, head_dim)
    up_frm = upstream.reshape(frames, -1, HEADS, head_dim)
    total = jnp.transpose(logsum.reshape(frames, -1, HEADS), (1, 2, 0))[..., None]
    scores = jnp.einsum("ibhd,jbhd->bhij", q_frm, k_frm, preferred_element_type=jnp.float32) * scale
    scores = jnp.where(allowed, scores, MASKED)
    probs = jnp.exp(scores - total)
    value_grad = jnp.einsum(
        "bhij,ibhd->jbhd", probs.astype(jnp.bfloat16), up_frm, preferred_element_type=jnp.float32
    )
    prob_grad = jnp.einsum("ibhd,jbhd->bhij", up_frm, v_frm, preferred_element_type=jnp.float32)
    score_grad = (probs * (prob_grad - jnp.sum(probs * prob_grad, axis=-1, keepdims=True))).astype(
        jnp.bfloat16
    )
    query_grad = (
        jnp.einsum("bhij,jbhd->ibhd", score_grad, k_frm, preferred_element_type=jnp.float32) * scale
    )
    key_grad = (
        jnp.einsum("bhij,ibhd->jbhd", score_grad, q_frm, preferred_element_type=jnp.float32) * scale
    )
    shape_two = (query.shape[0], query.shape[1])
    return jnp.concatenate(
        [query_grad.reshape(shape_two), key_grad.reshape(shape_two), value_grad.reshape(shape_two)],
        axis=1,
    )


def layer_forward(inputs, weights, live_rows, allowed, leading, window):
    (
        attention_gain,
        attention_bias,
        projection_in,
        projection_out,
        output_bias,
        feedforward_gain,
        feedforward_bias,
        up_weight,
        up_bias,
        down_weight,
        down_bias,
    ) = weights
    start = inputs.astype(jnp.float32)
    width = start.shape[1]
    normed = normalize(start, attention_gain, attention_bias).astype(jnp.bfloat16)
    joint = jnp.dot(normed, projection_in, preferred_element_type=jnp.float32).astype(jnp.bfloat16)
    query = joint[:, :width]
    keys = joint[:, width : 2 * width]
    values = joint[:, 2 * width :]
    scale = (width // HEADS) ** (-0.5)
    mixed, logsum = lax.cond(
        leading,
        partial(window_forward, scale=scale, window=window),
        partial(frame_forward, scale=scale, window=window),
        query,
        keys,
        values,
        allowed,
    )
    middle = start + (
        jnp.dot(mixed, projection_out, preferred_element_type=jnp.float32) + output_bias
    )
    normed_two = normalize(middle, feedforward_gain, feedforward_bias).astype(jnp.bfloat16)
    hidden_pre = jnp.dot(normed_two, up_weight, preferred_element_type=jnp.float32) + up_bias
    hidden = jax.nn.gelu(hidden_pre, approximate=False).astype(jnp.bfloat16)
    result = live_rows * (
        middle + (jnp.dot(hidden, down_weight, preferred_element_type=jnp.float32) + down_bias)
    )
    saved_state = (
        start,
        normed,
        query,
        keys,
        values,
        mixed,
        logsum,
        middle,
        normed_two,
        hidden_pre,
        hidden,
        live_rows,
        allowed,
    )
    return (result, saved_state)


def feedforward_backward(saved_state, weights, upstream):
    (
        start,
        normed,
        query,
        keys,
        values,
        mixed,
        logsum,
        middle,
        normed_two,
        hidden_pre,
        hidden,
        live_rows,
        allowed,
    ) = saved_state
    (
        attention_gain,
        attention_bias,
        projection_in,
        projection_out,
        output_bias,
        feedforward_gain,
        feedforward_bias,
        up_weight,
        up_bias,
        down_weight,
        down_bias,
    ) = weights
    outer = live_rows * upstream
    outer_low = outer.astype(jnp.bfloat16)
    down_bias_grad = jnp.sum(outer_low, axis=0, dtype=jnp.float32)
    down_weight_grad = jnp.einsum(
        "rf,rd->fd", hidden, outer_low, preferred_element_type=jnp.float32
    )
    hidden_grad = jnp.einsum(
        "rd,fd->rf", outer_low, down_weight, preferred_element_type=jnp.float32
    )
    unused, gelu_pull = jax.vjp(partial(jax.nn.gelu, approximate=False), hidden_pre)
    pre_grad = gelu_pull(hidden_grad)[0].astype(jnp.bfloat16)
    up_bias_grad = jnp.sum(pre_grad, axis=0, dtype=jnp.float32)
    up_weight_grad = jnp.einsum(
        "rd,rf->df", normed_two, pre_grad, preferred_element_type=jnp.float32
    )
    normed_grad = jnp.einsum("rf,df->rd", pre_grad, up_weight, preferred_element_type=jnp.float32)
    unused, norm_pull = jax.vjp(normalize, middle, feedforward_gain, feedforward_bias)
    middle_part, gain_grad, bias_grad = norm_pull(normed_grad)
    return (
        outer + middle_part,
        (gain_grad, bias_grad, up_weight_grad, up_bias_grad, down_weight_grad, down_bias_grad),
    )


def attention_backward(saved_state, weights, middle_grad, leading, window):
    (
        start,
        normed,
        query,
        keys,
        values,
        mixed,
        logsum,
        middle,
        normed_two,
        hidden_pre,
        hidden,
        live_rows,
        allowed,
    ) = saved_state
    (
        attention_gain,
        attention_bias,
        projection_in,
        projection_out,
        output_bias,
        feedforward_gain,
        feedforward_bias,
        up_weight,
        up_bias,
        down_weight,
        down_bias,
    ) = weights
    scale = (start.shape[1] // HEADS) ** (-0.5)
    branch_low = middle_grad.astype(jnp.bfloat16)
    output_bias_grad = jnp.sum(branch_low, axis=0, dtype=jnp.float32)
    projection_out_grad = jnp.einsum(
        "rd,re->de", mixed, branch_low, preferred_element_type=jnp.float32
    )
    mixed_grad = jnp.einsum(
        "re,de->rd", branch_low, projection_out, preferred_element_type=jnp.float32
    ).astype(jnp.bfloat16)
    joint_grad = lax.cond(
        leading,
        partial(window_backward, scale=scale, window=window),
        partial(frame_backward, scale=scale, window=window),
        query,
        keys,
        values,
        logsum,
        mixed_grad,
        allowed,
    ).astype(jnp.bfloat16)
    projection_in_grad = jnp.einsum(
        "rd,re->de", normed, joint_grad, preferred_element_type=jnp.float32
    )
    normed_grad = jnp.einsum(
        "re,de->rd", joint_grad, projection_in, preferred_element_type=jnp.float32
    )
    unused, norm_pull = jax.vjp(normalize, start, attention_gain, attention_bias)
    start_part, gain_grad, bias_grad = norm_pull(normed_grad)
    return (
        middle_grad + start_part,
        (gain_grad, bias_grad, projection_in_grad, projection_out_grad, output_bias_grad),
    )


def per_device(
    clip_tokens,
    window_cols,
    time_groups,
    cotangent,
    attention_gain,
    attention_bias,
    projection_in,
    projection_out,
    output_bias,
    feedforward_gain,
    feedforward_bias,
    up_weight,
    up_bias,
    down_weight,
    down_bias,
):
    leading = lax.axis_index("section") == 0
    micro = clip_tokens.shape[0]
    frames = clip_tokens.shape[2]
    band = clip_tokens.shape[3]
    width = clip_tokens.shape[4]
    row_count = frames * band
    window = band // WCAP
    weights = tuple(
        (
            weight[0]
            for weight in (
                attention_gain,
                attention_bias,
                projection_in,
                projection_out,
                output_bias,
                feedforward_gain,
                feedforward_bias,
                up_weight,
                up_bias,
                down_weight,
                down_bias,
            )
        )
    )
    slot_window = jnp.arange(row_count, dtype=jnp.int32) % band // window

    def masks_of(index):
        live_rows = (slot_window < window_cols[index, 0]).astype(jnp.float32)[:, None]
        labels = time_groups[index, 0]
        return (live_rows, labels[None, :] <= labels[:, None])

    def pick(early_part, later_part):
        return jax.tree.map(partial(jnp.where, leading), early_part, later_part)

    incoming = jnp.zeros((row_count, width), jnp.bfloat16)
    returning = jnp.zeros((row_count, width), jnp.bfloat16)
    forward_outs = []
    backward_outs = []
    history = []
    attention_totals = tuple((jnp.zeros(weight.shape, jnp.float32) for weight in weights[:5]))
    feedforward_totals = tuple((jnp.zeros(weight.shape, jnp.float32) for weight in weights[5:]))
    for step_index in range(micro + 2):
        if step_index <= micro:
            early_index = min(step_index, micro - 1)
            late_index = max(step_index - 1, 0)
            source = clip_tokens[early_index, 0].reshape(row_count, width)
            inputs = jnp.where(leading, source, incoming)
            live_rows, allowed = pick(masks_of(early_index), masks_of(late_index))
            result, saved_state = layer_forward(
                inputs, weights, live_rows, allowed, leading, window
            )
            result_low = result.astype(jnp.bfloat16)
            forward_outs.append(result_low)
            history.append(saved_state)
            if step_index < micro:
                incoming = shifted(result_low, "section", 1)
        if step_index >= 1:
            late_index = min(step_index - 1, micro - 1)
            saved_state = pick(history[max(step_index - 2, 0)], history[min(step_index, micro)])
            target = cotangent[late_index, 0].reshape(row_count, width).astype(jnp.float32)
            upstream = jnp.where(leading, returning.astype(jnp.float32), target)
            weighting = jnp.where(leading, float(step_index >= 2), float(step_index <= micro))
            middle_grad, feed_terms = feedforward_backward(saved_state, weights, upstream)
            feedforward_totals = tuple(
                (total + weighting * term for total, term in zip(feedforward_totals, feed_terms))
            )
            input_grad, attn_terms = attention_backward(
                saved_state, weights, middle_grad, leading, window
            )
            attention_totals = tuple(
                (total + weighting * term for total, term in zip(attention_totals, attn_terms))
            )
            input_low = input_grad.astype(jnp.bfloat16)
            backward_outs.append(input_low)
            if step_index <= micro:
                returning = shifted(input_low, "section", -1)
    attn_gain, attn_bias, attn_in, attn_out, attn_outbias = attention_totals
    feed_gain, feed_bias, feed_up, feed_upbias, feed_down, feed_downbias = feedforward_totals
    combined = lax.psum(
        (
            attn_gain,
            attn_bias,
            attn_in,
            attn_out,
            attn_outbias,
            feed_gain,
            feed_bias,
            feed_up,
            feed_upbias,
            feed_down,
            feed_downbias,
        ),
        "dp",
    )
    attention_totals = tuple(combined[:5])
    feedforward_totals = tuple(combined[5:])
    shape_out = (1, micro, 1, frames, band, width)
    activations = jnp.stack(
        [jnp.where(leading, forward_outs[index], forward_outs[index + 1]) for index in range(micro)]
    ).reshape(shape_out)
    input_grads = jnp.stack(
        [
            jnp.where(leading, backward_outs[index + 1], backward_outs[index])
            for index in range(micro)
        ]
    ).reshape(shape_out)
    gradients = tuple(
        (total[None] for total in tuple(attention_totals) + tuple(feedforward_totals))
    )
    return (activations, input_grads) + gradients


def solution(mesh):
    return jax.shard_map(
        per_device,
        mesh=mesh,
        in_specs=(
            P(None, "dp", None, None, None),
            P(None, "dp"),
            P(None, "dp", None),
            P(None, "dp", None, None, None),
            P("section", None),
            P("section", None),
            P("section", None, None),
            P("section", None, None),
            P("section", None),
            P("section", None),
            P("section", None),
            P("section", None, None),
            P("section", None),
            P("section", None, None),
            P("section", None),
        ),
        out_specs=(
            P("section", None, "dp", None, None, None),
            P("section", None, "dp", None, None, None),
            P("section", None),
            P("section", None),
            P("section", None, None),
            P("section", None, None),
            P("section", None),
            P("section", None),
            P("section", None),
            P("section", None, None),
            P("section", None),
            P("section", None, None),
            P("section", None),
        ),
        check_vma=False,
    )
```

profile of v0, /device:TPU:1, one launch (start us, length us, event | category | flops | bytes accessed | tf_op | source)
XLA Modules:
  0.0 1628.6 jit_solution(16881975272243675718)
XLA Ops:
  23.4 63.8 %conditional.21 = (bf16[1920,512]{0,1:T(8,128)(2,1)}, bf16[1920,512]{1,0:T(8,128)(2,1)}, f32[1920,8]{0,1:T(8,128)S(1)}) conditional(s32[]{:T(128)} %convert_element_type.343, (pred[6,6]{0,1:T(8,128)(4,1)}, bf16[1920,512]{1,0:T(8,128)(2,1)}, bf16[1920,512]{1,0:T(8,128)(2,1)}, bf16[1920,512]{1,0:T(8,128)(2,1)}) %tuple.80, (bf16[1920,512]{1,0:T(8,128)(2,1)}, ...), branch_computations={%region_2.5_spmd, %region_5.8_spmd} | conditional | flops 260628480 | bytes 59965492 | solution.py:145
  91.7 39.7 %fusion.233 = (bf16[1920,2048]{1,0:T(8,128)(2,1)S(1)}, f32[1920,2048]{1,0:T(8,128)}) fusion(f32[2048]{0:T(1024)S(1)} %bitcast.439, bf16[1,512,2048]{2,1,0:T(8,128)(2,1)S(1)} %copy-done, f32[1920,512]{1,0:T(8,128)S(1)} %get-tuple-element.501, f32[512]{0:T(512)S(1)} %bitcast.421, f32[512]{0:T(512)S(1)} %bitcast.397, f32[1920]{0:T(1024)S(1)} %add_rsqrt_fusion.5, ...), kind=kOutput, calls=%fused_computation.254 | convolution fusion | flops 4290969600 | bytes 29649920 | tf_op jit(solution)/shard_map/dot_general | solution.py:158
  137.0 28.5 %collective-permute-start = (bf16[1920,512]{1,0:T(8,128)(2,1)}, bf16[1920,512]{1,0:T(8,128)(2,1)}, u32[]{:S(2)}, u32[]{:S(2)}) collective-permute-start(bf16[1920,512]{1,0:T(8,128)(2,1)} %multiply_convert_fusion.9), channel_id=1, source_target_pairs={{0,16},{1,17},{2,18},{3,19},{4,20},{5,21},{6,22},{7,23},{8,24},{9,... | collective-permute-start | bytes 5898248 | tf_op jit(solution)/shard_map/ppermute | solution.py:19
  187.1 18.8 %collective-permute-done = bf16[1920,512]{1,0:T(8,128)(2,1)} collective-permute-done((bf16[1920,512]{1,0:T(8,128)(2,1)}, bf16[1920,512]{1,0:T(8,128)(2,1)}, u32[]{:S(2)}, u32[]{:S(2)}) %collective-permute-start) | collective-permute-done | bytes 1966112 | tf_op jit(solution)/shard_map/ppermute | solution.py:19
  219.6 63.7 %conditional.22 = (bf16[1920,512]{0,1:T(8,128)(2,1)}, bf16[1920,512]{1,0:T(8,128)(2,1)}, f32[1920,8]{0,1:T(8,128)S(1)}) conditional(s32[]{:T(128)} %convert_element_type.343, (pred[6,6]{0,1:T(8,128)(4,1)S(1)}, bf16[1920,512]{1,0:T(8,128)(2,1)}, bf16[1920,512]{1,0:T(8,128)(2,1)}, bf16[1920,512]{1,0:T(8,128)(2,1)}) %tuple.250, ...), branch_computations={%region_12.15_spmd, %region_15.18_spmd} | conditional | flops 260628480 | bytes 59965492 | solution.py:145
  294.0 40.4 %fusion.236 = (bf16[1920,2048]{1,0:T(8,128)(2,1)}, f32[1920,2048]{1,0:T(8,128)}) fusion(f32[2048]{0:T(1024)S(1)} %bitcast.440, bf16[1920,512]{1,0:T(8,128)(2,1)S(1)} %get-tuple-element.489, bf16[1,512,2048]{2,1,0:T(8,128)(2,1)S(1)} %copy-done), kind=kOutput, calls=%fused_computation.257 | convolution fusion | flops 4286054400 | bytes 27664384 | tf_op jit(solution)/shard_map/dot_general | solution.py:158
  334.5 45.6 %convert_reduce_fusion.2 = (f32[2048]{0:T(1024)}, bf16[1920,2048]{1,0:T(8,128)(2,1)S(1)}) fusion(bf16[1920,512]{1,0:T(8,128)(2,1)S(1)} %bitcast.388, bf16[1,2048,512]{2,1,0:T(8,128)(2,1)S(1)} %copy-done.197, f32[1920,2048]{1,0:T(8,128)} %get-tuple-element.507, f32[1920,2048]{1,0:T(8,128)} %get-tuple-element.503, f32[2048]{0:T(1024)S(1)} %bitcast.441, pred[]{:T(512)} %eq.5), kind=kOutput, calls=%fused_computation.278 | convolution fusion | flops 4329306112 | bytes 43401216 | tf_op jit(solution)/shard_map/rd,fd->rf/dot_general | solution.py:216
  410.7 27.5 %collective-permute-start.1 = (bf16[1920,512]{1,0:T(8,128)(2,1)}, bf16[1920,512]{1,0:T(8,128)(2,1)}, u32[]{:S(2)}, u32[]{:S(2)}) collective-permute-start(bf16[1920,512]{1,0:T(8,128)(2,1)} %get-tuple-element.515), channel_id=1, source_target_pairs={{0,16},{1,17},{2,18},{3,19},{4,20},{5,21},{6,22},{7,23},{8,24},{9,... | collective-permute-start | bytes 5898248 | tf_op jit(solution)/shard_map/ppermute | solution.py:19
  438.2 123.8 %conditional.24 = (bf16[1920,1536]{0,1:T(8,128)(2,1)}) conditional(s32[]{:T(128)} %convert_element_type.343, (pred[]{:T(512)}, pred[6,6]{0,1:T(8,128)(4,1)}, pred[6,6]{0,1:T(8,128)(4,1)S(1)}, bf16[1920,512]{1,0:T(8,128)(2,1)}, bf16[1920,512]{1,0:T(8,128)(2,1)}, /*index=5*/f32[1920,8]{0,1:T(8,128)S(1)}, bf16[1920,512]{1,0:T(8,128)(2,1)}, ...), branch_computations={%region_34.36_spmd, %region_36.38_spmd} | conditional | flops 662553600 | bytes 159805568
  476.8 11.2 copy.467
  494.2 12.4 multiply_reduce_fusion.4
  579.2 11.6 multiply_reduce_fusion.14
  605.2 63.6 %conditional.23 = (bf16[1920,512]{0,1:T(8,128)(2,1)}, bf16[1920,512]{1,0:T(8,128)(2,1)}, f32[1920,8]{0,1:T(8,128)S(1)}) conditional(s32[]{:T(128)} %convert_element_type.343, (pred[6,6]{0,1:T(8,128)(4,1)S(1)}, bf16[1920,512]{1,0:T(8,128)(2,1)}, bf16[1920,512]{1,0:T(8,128)(2,1)}, bf16[1920,512]{1,0:T(8,128)(2,1)}) %tuple.247, ...), branch_computations={%region_22.25_spmd, %region_25.28_spmd} | conditional | flops 260628480 | bytes 59965492 | solution.py:145
  689.0 40.4 %fusion.239 = (bf16[1920,2048]{1,0:T(8,128)(2,1)}, f32[1920,2048]{1,0:T(8,128)}) fusion(f32[2048]{0:T(1024)S(1)} %bitcast.442, bf16[1920,512]{1,0:T(8,128)(2,1)S(1)} %get-tuple-element.485, bf16[1,512,2048]{2,1,0:T(8,128)(2,1)S(1)} %copy-done), kind=kOutput, calls=%fused_computation.260 | convolution fusion | flops 4286054400 | bytes 27664384 | tf_op jit(solution)/shard_map/dot_general | solution.py:158
  733.0 71.9 %collective-permute-done.2 = bf16[1920,512]{1,0:T(8,128)(2,1)S(1)} collective-permute-done((bf16[1920,512]{1,0:T(8,128)(2,1)S(1)}, bf16[1920,512]{1,0:T(8,128)(2,1)S(1)}, u32[]{:S(2)}, u32[]{:S(2)}) %collective-permute-start.2) | collective-permute-done | bytes 1966112 | tf_op jit(solution)/shard_map/ppermute | solution.py:19
  806.4 46.4 %convert_reduce_fusion.1 = (f32[2048]{0:T(1024)}, bf16[1920,2048]{1,0:T(8,128)(2,1)S(1)}) fusion(bf16[1920,512]{1,0:T(8,128)(2,1)S(1)} %get-tuple-element.411, bf16[1,2048,512]{2,1,0:T(8,128)(2,1)S(1)} %copy-done.198, f32[1920,2048]{1,0:T(8,128)} %get-tuple-element.513, f32[1920,2048]{1,0:T(8,128)} %get-tuple-element.503, f32[2048]{0:T(1024)S(1)} %bitcast.443, ...), kind=kOutput, calls=%fused_computation.277 | convolution fusion | flops 4329306112 | bytes 43401216 | tf_op jit(solution)/shard_map/rd,fd->rf/dot_general | solution.py:216
  874.9 123.1 %conditional.25 = (bf16[1920,1536]{0,1:T(8,128)(2,1)}) conditional(s32[]{:T(128)} %convert_element_type.343, (pred[]{:T(512)}, pred[6,6]{0,1:T(8,128)(4,1)}, pred[6,6]{0,1:T(8,128)(4,1)S(1)}, bf16[1920,512]{1,0:T(8,128)(2,1)}, bf16[1920,512]{1,0:T(8,128)(2,1)}, /*index=5*/f32[1920,8]{0,1:T(8,128)S(1)}, bf16[1920,512]{1,0:T(8,128)(2,1)}, ...), branch_computations={%region_46.48_spmd, %region_48.50_spmd} | conditional | flops 662553600 | bytes 159805568
  913.3 11.2 copy.494
  930.7 12.3 multiply_reduce_fusion.6
  998.1 11.1 multiply_reduce_fusion.13
  1021.7 9.4 fusion.299
  1031.1 72.8 %collective-permute-done.3 = bf16[1920,512]{1,0:T(8,128)(2,1)S(1)} collective-permute-done((bf16[1920,512]{1,0:T(8,128)(2,1)S(1)}, bf16[1920,512]{1,0:T(8,128)(2,1)S(1)}, u32[]{:S(2)}, u32[]{:S(2)}) %collective-permute-start.3) | collective-permute-done | bytes 1966112 | tf_op jit(solution)/shard_map/ppermute | solution.py:19
  1105.3 46.0 %convert_reduce_fusion = (f32[2048]{0:T(1024)}, bf16[1920,2048]{1,0:T(8,128)(2,1)S(1)}) fusion(bf16[1920,512]{1,0:T(8,128)(2,1)S(1)} %get-tuple-element.413, bf16[1,2048,512]{2,1,0:T(8,128)(2,1)S(1)} %copy-done.199, f32[1920,2048]{1,0:T(8,128)} %get-tuple-element.513, f32[1920,2048]{1,0:T(8,128)} %get-tuple-element.507, f32[2048]{0:T(1024)S(1)} %bitcast.444, ...), kind=kOutput, calls=%fused_computation.276 | convolution fusion | flops 4329306112 | bytes 43401216 | tf_op jit(solution)/shard_map/rd,fd->rf/dot_general | solution.py:216
  1167.6 124.9 %conditional.26 = (bf16[1920,1536]{0,1:T(8,128)(2,1)}) conditional(s32[]{:T(128)} %convert_element_type.343, (pred[]{:T(512)}, pred[6,6]{0,1:T(8,128)(4,1)S(1)}, pred[6,6]{0,1:T(8,128)(4,1)S(1)}, bf16[1920,512]{1,0:T(8,128)(2,1)}, bf16[1920,512]{1,0:T(8,128)(2,1)}, /*index=5*/f32[1920,8]{0,1:T(8,128)S(1)}, bf16[1920,512]{1,0:T(8,128)(2,1)}, ...), branch_computations={%region_58.60_spmd, %region_60.62_spmd} | conditional | flops 662553600 | bytes 159805568
  1207.5 11.2 copy.521
  1224.8 12.3 multiply_reduce_fusion.8
  1292.5 10.5 convolution_multiply_fusion
  1303.1 12.1 add_bitcast_fusion
  1338.0 10.4 fusion.354
  1352.6 9.8 multiply_reduce_fusion.12
  1362.5 59.4 %all-reduce = (f32[1,512]{1,0:T(1,128)}, f32[1,512]{1,0:T(1,128)}, f32[1,512]{1,0:T(1,128)}, f32[1,512]{1,0:T(1,128)}, f32[1,512]{1,0:T(1,128)}, /*index=5*/f32[1,2048]{1,0:T(1,128)}, f32[1,512]{1,0:T(1,128)}) all-reduce(f32[1,512]{1,0:T(1,128)S(1)} %bitcast.431, ...), channel_id=1, replica_groups=mesh['section'=2,'dp'=16] {'dp'}, use_global_device_ids=true, to_apply=%region_69.70 | all-reduce | flops 5120 | bytes 40960 | tf_op jit(solution)/shard_map/psum | solution.py:393
  1432.0 178.6 %all-reduce.4.cloned.1.call-done = (f32[1,512,1536]{2,1,0:T(8,128)}, f32[1,512,512]{2,1,0:T(8,128)}, f32[1,512,2048]{2,1,0:T(8,128)}, f32[1,2048,512]{2,1,0:T(8,128)}) async-done(((f32[1,512,1536]{2,1,0:T(8,128)}, f32[1,512,512]{2,1,0:T(8,128)}, f32[1,512,2048]{2,1,0:T(8,128)}, f32[1,2048,512]{2,1,0:T(8,128)}), (f32[1,512,1536]{2,1,0:T(8,128)}, f32[1,512,512]{2,1,0:T(8,128)}, f32[1,512,2048]{2,1,0:T(8,128)}, ...) | async-done | bytes 12582928 | tf_op jit(solution)/shard_map/psum | solution.py:393
  (668 shorter events, 707.9 us)
Async XLA Ops:
  7.2 84.5 %copy-start = (bf16[1,512,2048]{2,1,0:T(8,128)(2,1)S(1)}, bf16[1,512,2048]{2,1,0:T(8,128)(2,1)}, u32[]{:S(2)}) copy-start(bf16[1,512,2048]{2,1,0:T(8,128)(2,1)} %param.38) | copy-start | bytes 6291460
  7.2 1603.4 %all-reduce.4.cloned.1.call-start = ((), (), s32[]{:S(2)}) async-start(), calls=%async_computation | async-start | bytes 25165824 | tf_op jit(solution)/shard_map/psum | solution.py:393
  23.4 63.8 %copy-start.77 = (bf16[1,512,512]{2,1,0:T(8,128)(2,1)S(1)}, bf16[1,512,512]{2,1,0:T(8,128)(2,1)}, u32[]{:S(2)}) copy-start(bf16[1,512,512]{2,1,0:T(8,128)(2,1)} %param.34) | copy-start | bytes 1572868
  23.4 63.8 %copy-start.207 = (f32[1,512]{1,0:T(1,128)S(1)}, f32[1,512]{1,0:T(1,128)}, u32[]{:S(2)}) copy-start(f32[1,512]{1,0:T(1,128)} %param.35) | copy-start | bytes 6148
  137.0 68.9 %collective-permute-start = (bf16[1920,512]{1,0:T(8,128)(2,1)}, bf16[1920,512]{1,0:T(8,128)(2,1)}, u32[]{:S(2)}, u32[]{:S(2)}) collective-permute-start(bf16[1920,512]{1,0:T(8,128)(2,1)} %multiply_convert_fusion.9), channel_id=1, source_target_pairs={{0,16},{1,17},{2,18},{3,19},{4,20},{5,21},{6,22},{7,23},{8,24},{9,... | collective-permute-start | bytes 5898248 | tf_op jit(solution)/shard_map/ppermute | solution.py:19
  219.6 63.7 %copy-start.208 = (f32[1,512]{1,0:T(1,128)S(1)}, f32[1,512]{1,0:T(1,128)}, u32[]{:S(2)}) copy-start(f32[1,512]{1,0:T(1,128)} %param.35) | copy-start | bytes 6148
  292.0 88.1 %copy-start.67 = (bf16[1920,512]{1,0:T(8,128)(2,1)}, bf16[1920,512]{1,0:T(8,128)(2,1)S(1)}, u32[]{:S(2)}) copy-start(bf16[1920,512]{1,0:T(8,128)(2,1)S(1)} %get-tuple-element.489) | copy-start | bytes 5898244
  410.7 165.8 %collective-permute-start.1 = (bf16[1920,512]{1,0:T(8,128)(2,1)}, bf16[1920,512]{1,0:T(8,128)(2,1)}, u32[]{:S(2)}, u32[]{:S(2)}) collective-permute-start(bf16[1920,512]{1,0:T(8,128)(2,1)} %get-tuple-element.515), channel_id=1, source_target_pairs={{0,16},{1,17},{2,18},{3,19},{4,20},{5,21},{6,22},{7,23},{8,24},{9,... | collective-permute-start | bytes 5898248 | tf_op jit(solution)/shard_map/ppermute | solution.py:19
  682.8 170.0 %copy-start.69 = (bf16[1920,512]{1,0:T(8,128)(2,1)}, bf16[1920,512]{1,0:T(8,128)(2,1)S(1)}, u32[]{:S(2)}) copy-start(bf16[1920,512]{1,0:T(8,128)(2,1)S(1)} %get-tuple-element.485) | copy-start | bytes 5898244
  687.7 117.2 %collective-permute-start.2 = (bf16[1920,512]{1,0:T(8,128)(2,1)S(1)}, bf16[1920,512]{1,0:T(8,128)(2,1)S(1)}, u32[]{:S(2)}, u32[]{:S(2)}) collective-permute-start(bf16[1920,512]{1,0:T(8,128)(2,1)S(1)} %add_convert_fusion.2), channel_id=1, source_target_pairs={{16,0},{17,1},{18,2},{19,3},{20,4},{21,5},{22,6},{23,7},{24,8},{25... | collective-permute-start | bytes 5898248 | tf_op jit(solution)/shard_map/ppermute | solution.py:19
  729.5 75.4 %copy-start.31 = (bf16[1,1,6,320,512]{4,3,2,1,0:T(8,128)(2,1)S(1)}, bf16[1,1,6,320,512]{4,3,2,1,0:T(8,128)(2,1)}, u32[]{:S(2)}) copy-start(bf16[1,1,6,320,512]{4,3,2,1,0:T(8,128)(2,1)} %slice.77) | copy-start | bytes 5898244
  729.5 75.4 %copy-start.109 = (f32[1920]{0:T(1024)S(1)}, f32[1920]{0:T(1024)}, u32[]{:S(2)}) copy-start(f32[1920]{0:T(1024)} %convert_select_fusion.7) | copy-start | bytes 23044
  731.1 121.6 %copy-start.114 = (f32[1920]{0:T(1024)}, f32[1920]{0:T(1024)S(1)}, u32[]{:S(2)}) copy-start(f32[1920]{0:T(1024)S(1)} %multiply_reduce_fusion.18) | copy-start | bytes 23044
  731.1 75.2 %copy-start.198 = (bf16[1,2048,512]{2,1,0:T(8,128)(2,1)S(1)}, bf16[1,2048,512]{2,1,0:T(8,128)(2,1)}, u32[]{:S(2)}) copy-start(bf16[1,2048,512]{2,1,0:T(8,128)(2,1)} %param.40) | copy-start | bytes 6291460
  874.8 123.2 %copy-start.126 = (f32[1,512]{1,0:T(1,128)S(1)}, f32[1,512]{1,0:T(1,128)}, u32[]{:S(2)}) copy-start(f32[1,512]{1,0:T(1,128)} %param.31) | copy-start | bytes 6148
  874.8 123.2 %copy-start.134 = (f32[1920]{0:T(1024)S(1)}, f32[1920]{0:T(1024)}, u32[]{:S(2)}) copy-start(f32[1920]{0:T(1024)} %copy-done.133) | copy-start | bytes 23044
  874.8 123.2 %copy-start.138 = (f32[1920]{0:T(1024)S(1)}, f32[1920]{0:T(1024)}, u32[]{:S(2)}) copy-start(f32[1920]{0:T(1024)} %get-tuple-element.529) | copy-start | bytes 23044
  874.8 123.2 %copy-start.140 = (f32[1920]{0:T(1024)S(1)}, f32[1920]{0:T(1024)}, u32[]{:S(2)}) copy-start(f32[1920]{0:T(1024)} %get-tuple-element.528) | copy-start | bytes 23044
  874.8 123.2 %copy-start.165 = (f32[1920]{0:T(1024)S(1)}, f32[1920]{0:T(1024)}, u32[]{:S(2)}) copy-start(f32[1920]{0:T(1024)} %div.228) | copy-start | bytes 23044
  874.9 123.2 %copy-start.166 = (f32[1920]{0:T(1024)S(1)}, f32[1920]{0:T(1024)}, u32[]{:S(2)}) copy-start(f32[1920]{0:T(1024)} %rsqrt.124) | copy-start | bytes 23044
  874.9 123.2 %copy-start.184 = (f32[1,512]{1,0:T(1,128)S(1)}, f32[1,512]{1,0:T(1,128)}, u32[]{:S(2)}) copy-start(f32[1,512]{1,0:T(1,128)} %param.32) | copy-start | bytes 6148
  1020.2 83.7 %collective-permute-start.3 = (bf16[1920,512]{1,0:T(8,128)(2,1)S(1)}, bf16[1920,512]{1,0:T(8,128)(2,1)S(1)}, u32[]{:S(2)}, u32[]{:S(2)}) collective-permute-start(bf16[1920,512]{1,0:T(8,128)(2,1)S(1)} %get-tuple-element.421), channel_id=1, source_target_pairs={{16,0},{17,1},{18,2},{19,3},{20,4},{21,5},{22,6},{23,7},{24,8},{25... | collective-permute-start | bytes 5898248 | tf_op jit(solution)/shard_map/ppermute | solution.py:19
  1021.7 82.2 %copy-start.32 = (bf16[1,1,6,320,512]{4,3,2,1,0:T(8,128)(2,1)S(1)}, bf16[1,1,6,320,512]{4,3,2,1,0:T(8,128)(2,1)}, u32[]{:S(2)}) copy-start(bf16[1,1,6,320,512]{4,3,2,1,0:T(8,128)(2,1)} %slice.77) | copy-start | bytes 5898244
  1021.7 82.2 %copy-start.108 = (f32[1920]{0:T(1024)S(1)}, f32[1920]{0:T(1024)}, u32[]{:S(2)}) copy-start(f32[1920]{0:T(1024)} %convert_select_fusion.6) | copy-start | bytes 23044
  1031.1 74.1 %copy-start.199 = (bf16[1,2048,512]{2,1,0:T(8,128)(2,1)S(1)}, bf16[1,2048,512]{2,1,0:T(8,128)(2,1)}, u32[]{:S(2)}) copy-start(bf16[1,2048,512]{2,1,0:T(8,128)(2,1)} %param.40) | copy-start | bytes 6291460
  1031.1 74.1 %copy-start.206 = (f32[1,2048]{1,0:T(1,128)S(1)}, f32[1,2048]{1,0:T(1,128)}, u32[]{:S(2)}) copy-start(f32[1,2048]{1,0:T(1,128)} %param.39) | copy-start | bytes 24580
  1167.6 124.9 %copy-start.127 = (f32[1,512]{1,0:T(1,128)S(1)}, f32[1,512]{1,0:T(1,128)}, u32[]{:S(2)}) copy-start(f32[1,512]{1,0:T(1,128)} %param.31) | copy-start | bytes 6148
  1167.6 124.9 %copy-start.129 = (f32[1920]{0:T(1024)S(1)}, f32[1920]{0:T(1024)}, u32[]{:S(2)}) copy-start(f32[1920]{0:T(1024)} %copy-done.128) | copy-start | bytes 23044
  1167.6 124.9 %copy-start.164 = (f32[1920]{0:T(1024)S(1)}, f32[1920]{0:T(1024)}, u32[]{:S(2)}) copy-start(f32[1920]{0:T(1024)} %copy-done.163) | copy-start | bytes 23044
  1167.6 124.9 %copy-start.172 = (f32[1920]{0:T(1024)S(1)}, f32[1920]{0:T(1024)}, u32[]{:S(2)}) copy-start(f32[1920]{0:T(1024)} %copy-done.170) | copy-start | bytes 23044
  1167.6 124.9 %copy-start.175 = (f32[1920]{0:T(1024)S(1)}, f32[1920]{0:T(1024)}, u32[]{:S(2)}) copy-start(f32[1920]{0:T(1024)} %copy-done.173) | copy-start | bytes 23044
  1167.6 124.9 %copy-start.185 = (f32[1,512]{1,0:T(1,128)S(1)}, f32[1,512]{1,0:T(1,128)}, u32[]{:S(2)}) copy-start(f32[1,512]{1,0:T(1,128)} %param.32) | copy-start | bytes 6148
  (195 other events, 2571.1 us)
Sparse Core Ops, SparseCore 0:
  1337.5 273.1 all-reduce.3
where the time goes:
time: 1640 us; the launch traced here: 1630 us
  matrix products  591 us (36%)
  local copies, waits for them, and re-layouts  386 us (24%)
  waiting for transfers between devices  342 us (21%)
  other arithmetic  132 us (8%)
  blocking collectives  59.4 us (4%)
  starting transfers between devices  58.9 us (4%)
  loops' own time  42.2 us (3%)
  between operations  17.1 us (1%)
    psum x1, waiting for transfers between devices, per_device(): lax.psum((attn_gain, attn_bias, attn_in, attn_out, attn_outbias, feed_gai...  179 us
    ppermute x4, waiting for transfers between devices, shifted(): lax.ppermute(value, axis, [(source, source + steps) for source in range(i...  163 us
    dot_general x3, matrix products, feedforward_backward(): jnp.einsum('rd,fd->rf', outer_low, down_weight, preferred_element_type=jn...  138 us
    dot_general x3, matrix products, layer_forward(): jnp.dot(normed_two, up_weight, preferred_element_type=jnp.float32) + up_bias  121 us
    psum x1, blocking collectives, per_device(): lax.psum((attn_gain, attn_bias, attn_in, attn_out, attn_outbias, feed_gai...  59.4 us
    ppermute x4, starting transfers between devices, shifted(): lax.ppermute(value, axis, [(source, source + steps) for source in range(i...  58.8 us
    another operation x30, local copies, waits for them, and re-layouts  41.2 us
    dot_general x3, matrix products, window_backward(): jnp.einsum('gqhd,gkhd->ghqk', up_win, v_win, preferred_element_type=jnp.f...  37 us
  transfers between devices with their start and end apart: 5, of which 4 were waited for; matrix products, arithmetic and copies ran while one was open for 15% of the time, Pallas kernels for 0%

commit v1 on v0

v1 whole, which is shorter than its diff:
```python
from collections import namedtuple
from functools import partial

import jax
import jax.numpy as jnp
from jax import lax
from jax.experimental import pallas as pl
from jax.experimental.pallas import tpu as pltpu
from jax.sharding import PartitionSpec as P

HEADS = 8
WCAP = 5
EPSILON = 1e-05
MASKED = -1e30
MESH = pl.DeviceIdType.MESH

F32 = jnp.float32
BF16 = jnp.bfloat16

LEAD = 4
SLOTS = LEAD + 1
Kept = namedtuple("Kept", ("x", "a1t", "qkv", "p", "ot", "xh2", "a2t", "rs2", "h", "g"))
FF_BLOCK = 512
ROWS_AT_ONCE = 32
COLS_AT_ONCE = 256

INV_SQRT2 = 0.7071067811865476
PDF = 0.3989422804014327
LOG2E = 1.4426950408889634


def mm(a, b):
    return lax.dot_general(a, b, (((1,), (0,)), ((), ())), preferred_element_type=F32)


def mm_bt(a, b):
    return lax.dot_general(a, b, (((1,), (1,)), ((), ())), preferred_element_type=F32)


def mm_at(a, b):
    return lax.dot_general(a, b, (((0,), (0,)), ((), ())), preferred_element_type=F32)


def gelu_and_slope(u):
    cdf = 0.5 + 0.5 * lax.erf(INV_SQRT2 * u)
    bell = jnp.exp2((-0.5 * LOG2E) * (u * u))
    return u * cdf, cdf + (PDF * u) * bell


def fold8(values):
    rows, cols = values.shape
    return jnp.sum(values.reshape(rows // 8, 8, cols), axis=0)


GROUP = 16
LINE = 4
LINE_ORDER = (3, 0, 2, 1)
UNIT = 384
PIECE = 128
WHOLE = slice(0, UNIT)
ACROSS_FIRST = slice(0, 256)
LINE_FIRST = slice(256, UNIT)
PART = {1: ACROSS_FIRST, 2: LINE_FIRST}
SIDES = {1: (0,), 2: (0, 1)}
FAMILIES = 32
VECTOR_ROWS = 16


def group_place():
    me = lax.axis_index("dp")
    core, across, line = lax.rem(me, 2), lax.rem(lax.div(me, 2), 2), lax.rem(lax.div(me, 4), LINE)
    sibling, beside = {"dp": me + 1 - 2 * core}, {"dp": me + 2 - 4 * across}
    return core, across, line, sibling, beside, {"dp": me + 4}, {"dp": me - 4}


def sum_over_group(packed, result, landing, vector, flat_ref, vector_ref, send_sem, recv_sem, out_sem, ready):
    core, across, line, sibling, beside, above, below = group_place()
    sides = (across, 1 - across)
    families = {}
    pending = []

    def when(condition, action):
        if condition is None:
            action()
        else:
            pl.when(condition)(action)

    def remote(family, place, source, target, device):
        number = families.setdefault(family, len(families)) * LINE + place
        return pltpu.make_async_remote_copy(
            src_ref=source,
            dst_ref=target,
            send_sem=send_sem.at[number],
            recv_sem=recv_sem.at[number],
            device_id=device,
            device_id_type=MESH,
        )

    def start(family, place, source, target, device):
        remote(family, place, source, target, device).start()

    def sent(family, place, source, device, condition=None):
        pending.append((condition, lambda: remote(family, place, source, source, device).wait_send()))

    def received(family, place, target, device):
        remote(family, place, target, target, device).wait_recv()

    def unit(ref, half, side, place, part):
        column = place * 512 if isinstance(place, int) else pl.multiple_of(place * 512, 512)
        return ref.at[half * 2 + side, part, pl.ds(column, 512)]

    def add(target, arrived):
        for r in range(0, target.shape[0], 64):
            at = slice(r, r + 64)
            target[at] = (target[at].astype(F32) + arrived[at].astype(F32)).astype(BF16)

    def store(far, rel, place, kind):
        half, side, part = (1 - core if far else core), sides[rel], PART[kind]
        row = pl.multiple_of(((half * 2 + side) * LINE + place) * UNIT + part.start, PIECE)
        return pltpu.make_async_copy(
            unit(result, half, side, place, part),
            flat_ref.at[pl.ds(row, part.stop - part.start)],
            out_sem.at[((far * 2 + rel) * 2 + kind - 1) * LINE + place],
        )

    for number, (device, condition) in enumerate(
        ((sibling, None), (beside, None), (below, line > 0), (above, line < LINE - 1))
    ):
        there = number if number < 2 else 5 - number
        when(
            condition,
            partial(pl.semaphore_signal, ready.at[there], inc=1, device_id=device, device_id_type=MESH),
        )
    pl.semaphore_wait(ready.at[0], 1)

    start("vector core", 0, vector.at[0], vector.at[1], sibling)
    sent("vector core", 0, vector.at[0], sibling)
    for place in LINE_ORDER:
        for side in range(2):
            source = unit(packed, 1 - core, side, place, WHOLE)
            start(("core", side), place, source, landing("core", side, place), sibling)
            sent(("core", side), place, source, sibling)
    pl.semaphore_wait(ready.at[1], 1)
    pl.when(line > 0)(lambda: pl.semaphore_wait(ready.at[2], 1))
    pl.when(line < LINE - 1)(lambda: pl.semaphore_wait(ready.at[3], 1))

    def line_send(kind, place, up, condition):
        device = above if up else below

        def go():
            for rel in SIDES[kind]:
                source = unit(packed, core, sides[rel], place, PART[kind])
                start((kind, up, rel), place, source, landing((kind, up), rel, place), device)

        pl.when(condition)(go)
        for rel in SIDES[kind]:
            sent((kind, up, rel), place, unit(packed, core, sides[rel], place, PART[kind]), device, condition)

    def line_take(kind, place, up, condition):
        def go():
            for rel in SIDES[kind]:
                spot = landing((kind, up), rel, place)
                received((kind, up, rel), place, spot, below if up else above)
                add(unit(packed, core, sides[rel], place, PART[kind]), spot)

        pl.when(condition)(go)

    def from_ends(kind, place):
        if place > 0:
            line_send(kind, place, True, line == 0)
        if place < LINE - 1:
            line_send(kind, place, False, line == LINE - 1)

    def inner_step(kind, k):
        place = LINE - 1 - k
        line_take(kind, place, True, (line > 0) & (line <= place))
        if place > 1:
            line_send(kind, place, True, (line > 0) & (line < place))
        place = k
        line_take(kind, place, False, (line < LINE - 1) & (line >= place))
        if place < LINE - 2:
            line_send(kind, place, False, (line < LINE - 1) & (line > place))

    def take_across(place):
        spot = landing("across", 0, place)
        received("across", place, spot, beside)
        add(unit(packed, core, sides[0], place, ACROSS_FIRST), spot)
        from_ends(1, place)

    for place in LINE_ORDER:
        for side in range(2):
            spot = landing("core", side, place)
            received(("core", side), place, spot, sibling)
            add(unit(packed, core, side, place, WHOLE), spot)
        source = unit(packed, core, sides[1], place, ACROSS_FIRST)
        start("across", place, source, landing("across", 0, place), beside)
        sent("across", place, source, beside)
        from_ends(2, place)
    received("vector core", 0, vector.at[1], sibling)
    vector[2] = vector[0] + vector[1]
    start("vector across", 0, vector.at[2], vector.at[3], beside)
    sent("vector across", 0, vector.at[2], beside)
    for k in range(LINE - 1):
        take_across(LINE_ORDER[k])
        inner_step(2, k)
    take_across(LINE_ORDER[LINE - 1])
    source = unit(packed, core, sides[1], line, LINE_FIRST)
    start("across 2", 0, source, landing("across 2", 0, 0), beside)
    sent("across 2", 0, source, beside)
    received("vector across", 0, vector.at[3], beside)
    vector[4 + line] = vector[2] + vector[3]
    inner_step(1, 0)
    inner_step(1, 1)
    spot = landing("across 2", 0, 0)
    received("across 2", 0, spot, beside)
    own = unit(packed, core, sides[0], line, LINE_FIRST)
    add(own, spot)
    own_two = unit(result, core, sides[0], line, LINE_FIRST)
    own_two[...] = own[...]
    start("gather across 2", 0, own_two, own_two, beside)
    sent("gather across 2", 0, own_two, beside)
    inner_step(1, 2)
    own_one = unit(result, core, sides[0], line, ACROSS_FIRST)
    own_one[...] = unit(packed, core, sides[0], line, ACROSS_FIRST)[...]

    def spread(family, place, spot, up, down):
        if up is not None:
            pl.when(up)(lambda: start((family, True), place, spot, spot, above))
        if down is not None:
            pl.when(down)(lambda: start((family, False), place, spot, spot, below))

    def hand_over(kind, rel, place):
        spot = unit(result, core, sides[rel], place, PART[kind])
        start(("gather core", kind, rel), place, spot, spot, sibling)
        store(0, rel, place, kind).start()

    def have(kind, rel, place, up, down):
        spot = unit(result, core, sides[rel], place, PART[kind])
        spread(("spread", kind, rel), place, spot, up, down)
        if kind == 1:
            start("gather across", place, spot, spot, beside)
        hand_over(kind, rel, place)

    def come(distance, action):
        pl.when(line >= distance)(lambda: action(line - distance, True))
        pl.when(line + distance < LINE)(lambda: action(line + distance, False))

    def arrive(kind, rel, distance):
        def action(place, up):
            spot = unit(result, core, sides[rel], place, PART[kind])
            received((("spread", kind, rel), up), place, spot, below if up else above)
            have(kind, rel, place, line < LINE - 1 if up else None, None if up else line > 0)

        come(distance, action)

    def arrive_vector(distance):
        def action(place, up):
            spot = vector.at[4 + place]
            received(("vector", up), place, spot, below if up else above)
            spread("vector", place, spot, line < LINE - 1 if up else None, None if up else line > 0)

        come(distance, action)

    def arrive_across(distance):
        def action(place, up):
            received("gather across", place, unit(result, core, sides[1], place, ACROSS_FIRST), beside)
            hand_over(1, 1, place)

        if distance == 0:
            action(line, True)
        else:
            come(distance, action)

    have(1, 0, line, line < LINE - 1, line > 0)
    have(2, 0, line, line < LINE - 1, line > 0)
    spread("vector", line, vector.at[4 + line], line < LINE - 1, line > 0)
    received("gather across 2", 0, unit(result, core, sides[1], line, LINE_FIRST), beside)
    have(2, 1, line, line < LINE - 1, line > 0)
    for distance in range(1, LINE):
        arrive(1, 0, distance)
        arrive(2, 0, distance)
        arrive(2, 1, distance)
        arrive_vector(distance)
        arrive_across(distance - 1)
    arrive_across(LINE - 1)
    vector[1] = (vector[4] + vector[5]) + (vector[6] + vector[7])
    vector_out = pltpu.make_async_copy(vector.at[1], vector_ref, out_sem.at[2 * GROUP])
    vector_out.start()
    for place in range(LINE):
        for kind in (1, 2):
            for rel in range(2):
                spot = unit(result, 1 - core, sides[rel], place, PART[kind])
                received(("gather core", kind, rel), place, spot, sibling)
                store(1, rel, place, kind).start()
    vector_out.wait()

    for place in range(LINE):
        for kind in (1, 2):
            for rel in range(2):
                spot = unit(result, core, sides[rel], place, PART[kind])
                sent(("gather core", kind, rel), place, spot, sibling)
                store(0, rel, place, kind).wait()
                store(1, rel, place, kind).wait()
            for rel in SIDES[kind]:
                spot = unit(result, core, sides[rel], place, PART[kind])
                sent((("spread", kind, rel), True), place, spot, above, (line >= place) & (line < LINE - 1))
                sent((("spread", kind, rel), False), place, spot, below, (line <= place) & (line > 0))
        sent("gather across", place, unit(result, core, sides[0], place, ACROSS_FIRST), beside)
        sent(("vector", True), place, vector.at[4 + place], above, (line >= place) & (line < LINE - 1))
        sent(("vector", False), place, vector.at[4 + place], below, (line <= place) & (line > 0))
    for condition, wait in pending:
        when(condition, wait)


def relay_kernel(
    dims,
    cols_ref,
    groups_ref,
    clip_ref,
    cot_ref,
    attention_gain,
    attention_bias,
    projection_in,
    projection_out,
    output_bias,
    feedforward_gain,
    feedforward_bias,
    up_weight,
    up_bias,
    down_weight,
    down_bias,
    act_ref,
    grad_ref,
    flat_ref,
    vector_ref,
    *scratch,
):
    micro, frames, window, width, hidden, grouped = dims
    parked, scratch = scratch[: len(Kept._fields) - 1], scratch[len(Kept._fields) - 1 :]
    kept_a, scratch = Kept(*scratch[: len(Kept._fields)]), scratch[len(Kept._fields) :]
    kept_b, scratch = Kept(*scratch[: len(Kept._fields)]), scratch[len(Kept._fields) :]
    (
    d_projection_in,
    d_projection_out,
    d_up_weight,
    d_down_weight,
    xbuf,
    dybuf,
    ybuf,
    dxbuf,
    a1_buf,
    pf_buf,
    ds_buf,
    o_buf,
    a2_buf,
    wide,
    total,
    u_buf,
    e_buf,
    et_buf,
    c_buf,
    do_buf,
    dqkv_buf,
    qkvt_buf,
    dot_buf,
    dqkvt_buf,
    sum_ag,
    sum_ab,
    sum_ob,
    sum_fg,
    sum_fb,
    sum_ub,
    sum_db,
    x_sem,
    dy_sem,
    y_sem,
    y_send,
    dx_sem,
    dx_send,
    packed,
    result,
    park_sem,
    fetch_sem,
    vector,
    group_send,
    group_recv,
    group_out,
    ready,
    ) = scratch
    rows = frames * window
    count = micro * WCAP
    head = width // HEADS
    pair = 2 * head
    scale = head ** (-0.5)
    section = lax.axis_index("section")
    leading = section == 0
    trailing = section != 0
    lead = LEAD * (1 - section)
    partner = {"section": 1 - section}

    def hbm_chunk(ref, chunk):
        start = pl.multiple_of(lax.rem(chunk, WCAP) * window, window)
        return ref.at[lax.div(chunk, WCAP), :, pl.ds(start, window), :]

    def x_load(chunk):
        slot = lax.rem(chunk, SLOTS)
        return pltpu.make_async_copy(hbm_chunk(clip_ref, chunk), xbuf.at[slot], x_sem.at[slot])

    def dy_load(chunk):
        slot = lax.rem(chunk, SLOTS)
        return pltpu.make_async_copy(hbm_chunk(cot_ref, chunk), dybuf.at[slot], dy_sem.at[slot])

    def y_store(chunk):
        slot = lax.rem(chunk, 2)
        return pltpu.make_async_copy(ybuf.at[slot], hbm_chunk(act_ref, chunk), y_sem.at[slot])

    def dx_store(chunk):
        slot = lax.rem(chunk, 2)
        return pltpu.make_async_copy(dxbuf.at[slot], hbm_chunk(grad_ref, chunk), dx_sem.at[slot])

    def park(chunk):
        slot = lax.rem(chunk, SLOTS)
        return [
            pltpu.make_async_copy(here, there.at[slot], park_sem.at[n])
            for n, (here, there) in enumerate(zip(kept_a[1:], parked))
        ]

    def fetch(chunk):
        slot = lax.rem(chunk, SLOTS)
        return [pltpu.make_async_copy(hbm_chunk(clip_ref, chunk), kept_b.x, fetch_sem.at[0])] + [
            pltpu.make_async_copy(there.at[slot], here, fetch_sem.at[n + 1])
            for n, (here, there) in enumerate(zip(kept_b[1:], parked))
        ]

    def start_all(copies):
        for copy in copies:
            copy.start()

    def wait_all(copies):
        for copy in copies:
            copy.wait()

    def y_remote(chunk):
        slot, there = lax.rem(chunk, 2), lax.rem(chunk, SLOTS)
        return pltpu.make_async_remote_copy(
            src_ref=ybuf.at[slot],
            dst_ref=xbuf.at[there],
            send_sem=y_send.at[slot],
            recv_sem=x_sem.at[there],
            device_id=partner,
            device_id_type=MESH,
        )

    def dx_remote(chunk):
        slot, there = lax.rem(chunk, 2), lax.rem(chunk, SLOTS)
        return pltpu.make_async_remote_copy(
            src_ref=dxbuf.at[slot],
            dst_ref=dybuf.at[there],
            send_sem=dx_send.at[slot],
            recv_sem=dy_sem.at[there],
            device_id=partner,
            device_id_type=MESH,
        )

    barrier = pltpu.get_barrier_semaphore()
    greeted = 1
    pl.semaphore_signal(barrier, inc=1, device_id=partner, device_id_type=MESH)
    if grouped:
        _, _, line, sibling, beside, above, below = group_place()
        has_below, has_above = line > 0, line < LINE - 1
        for device, condition in ((sibling, None), (beside, None), (below, has_below), (above, has_above)):
            greet = partial(pl.semaphore_signal, barrier, inc=1, device_id=device, device_id_type=MESH)
            if condition is None:
                greet()
            else:
                pl.when(condition)(greet)
        greeted = 3 + has_below.astype(jnp.int32) + has_above.astype(jnp.int32)

    @pl.when(leading)
    def _():
        x_load(0).start()

    @pl.when(trailing)
    def _():
        dy_load(0).start()

    for total_ref in (d_projection_in, d_projection_out, d_up_weight, d_down_weight):
        total_ref[...] = jnp.zeros_like(total_ref)
    for total_ref in (sum_ag, sum_ab, sum_ob, sum_fg, sum_fb, sum_ub, sum_db):
        total_ref[...] = jnp.zeros_like(total_ref)

    pl.semaphore_wait(barrier, greeted)

    def frame_rows(i):
        return slice(i * window, (i + 1) * window)

    half = lax.broadcasted_iota(jnp.int32, (window, pair), 1) < head
    low_half = jnp.where(half, 1.0, 0.0).astype(BF16)
    high_half = jnp.where(half, 0.0, 1.0).astype(BF16)

    def by_head(values):
        return jnp.concatenate([values * low_half, values * high_half], axis=0)

    def join_heads(values):
        return jnp.where(half, values[:window], values[window:])

    heads_of = [
        (frame_rows(f), slice(n * pair, (n + 1) * pair), n) for f in range(frames) for n in range(width // pair)
    ]

    def of_pair(ref, at, which, n):
        return ref[at, which * width + n * pair : which * width + (n + 1) * pair]

    def window_forward(kept):
        for at, lanes, n in heads_of:
            keys = of_pair(kept.qkv, at, 1, n)
            total[at, lanes] = mm_bt(keys, by_head(of_pair(kept.qkv, at, 0, n)))
        yield
        for at, lanes, n in heads_of:
            scores = total[at, lanes] * scale
            scores = jnp.exp(scores - jnp.max(scores, axis=0, keepdims=True))
            probs = scores * (1.0 / jnp.sum(scores, axis=0, keepdims=True))
            kept.p[at, lanes] = probs.astype(BF16)
        yield
        for at, lanes, n in heads_of:
            values = of_pair(kept.qkv, at, 2, n)
            o_buf[at, lanes] = join_heads(mm_at(kept.p[at, lanes], values)).astype(BF16)

    def window_backward(kept):
        for at, lanes, n in heads_of:
            up = by_head(do_buf[at, lanes])
            total[at, lanes] = mm_bt(of_pair(kept.qkv, at, 2, n), up)
            dv = mm(kept.p[at, lanes], up)
            dqkv_buf[at, 2 * width + n * pair : 2 * width + (n + 1) * pair] = dv.astype(BF16)
        yield
        for at, lanes, n in heads_of:
            probs = kept.p[at, lanes].astype(F32)
            dp = total[at, lanes]
            ds = probs * (dp - jnp.sum(probs * dp, axis=0, keepdims=True))
            e_buf[at, lanes] = ds.astype(BF16)
        yield
        for at, lanes, n in heads_of:
            ds = e_buf[at, lanes]
            dk = mm(ds, by_head(of_pair(kept.qkv, at, 0, n))) * scale
            dqkv_buf[at, width + n * pair : width + (n + 1) * pair] = dk.astype(BF16)
            dq = join_heads(mm_at(ds, of_pair(kept.qkv, at, 1, n))) * scale
            dqkv_buf[at, lanes] = dq.astype(BF16)

    low_frame = lax.broadcasted_iota(jnp.int32, (1, 128), 1) < window

    def lane_tiles(i):
        return min(i + 1, frames - 1) // 2 + 1

    def tile(t):
        return slice(t * 128, (t + 1) * 128)

    def head_rows(which, h):
        return slice(which * width + h * head, which * width + (h + 1) * head)

    def other_half(values):
        return pltpu.roll(values, window, axis=1)

    def both_frames(ref, at, t):
        values = ref[at, tile(t)]
        turned = other_half(values)
        return jnp.where(low_frame, values, turned), jnp.where(low_frame, turned, values)

    def frame_forward(chunk, kept):
        tile_count = frames // 2
        for n in range(3):
            flat = kept.qkv[:, n * width : (n + 1) * width].T
            qkvt_buf[n * width : (n + 1) * width, :] = flat.astype(F32)
        for h in range(HEADS):
            keys = [qkvt_buf[head_rows(1, h), tile(t)] for t in range(tile_count)]
            for pair_index in range(tile_count):
                queries = both_frames(qkvt_buf, head_rows(0, h), pair_index)
                for i in (2 * pair_index, 2 * pair_index + 1):
                    for t in range(lane_tiles(i)):
                        score = jnp.sum(queries[i % 2] * keys[t], axis=0, keepdims=True)
                        ds_buf[i * tile_count + t, h : h + 1, :] = score
        yield
        item = lax.div(chunk, WCAP)
        labels = [
            jnp.where(low_frame, groups_ref[item, 0, 2 * t], groups_ref[item, 0, 2 * t + 1])
            for t in range(tile_count)
        ]
        for i in range(frames):
            mine = groups_ref[item, 0, i]
            parts = [
                jnp.where(labels[t] <= mine, ds_buf[i * tile_count + t] * scale, MASKED)
                for t in range(lane_tiles(i))
            ]
            largest = parts[0]
            for part in parts[1:]:
                largest = jnp.maximum(largest, part)
            largest = jnp.maximum(largest, other_half(largest))
            parts = [jnp.exp(part - largest) for part in parts]
            whole = parts[0]
            for part in parts[1:]:
                whole = whole + part
            whole = 1.0 / (whole + other_half(whole))
            for t, part in enumerate(parts):
                pf_buf[i * tile_count + t] = part * whole
        yield
        for h in range(HEADS):
            values = [qkvt_buf[head_rows(2, h), tile(t)] for t in range(tile_count)]
            for pair_index in range(tile_count):
                mixed = []
                for i in (2 * pair_index, 2 * pair_index + 1):
                    part = 0.0
                    for t in range(lane_tiles(i)):
                        part = part + pf_buf[i * tile_count + t, h : h + 1, :] * values[t]
                    mixed.append(part + other_half(part))
                both = jnp.where(low_frame, mixed[0], mixed[1])
                kept.ot[head_rows(0, h), tile(pair_index)] = both.astype(BF16)

    def frame_backward(kept):
        tile_count = frames // 2
        for h in range(HEADS):
            values = [qkvt_buf[head_rows(2, h), tile(t)] for t in range(tile_count)]
            dv = [0.0] * tile_count
            for pair_index in range(tile_count):
                ups = both_frames(dot_buf, head_rows(0, h), pair_index)
                for i in (2 * pair_index, 2 * pair_index + 1):
                    for t in range(lane_tiles(i)):
                        ds_buf[i * tile_count + t, h : h + 1, :] = jnp.sum(
                            ups[i % 2] * values[t], axis=0, keepdims=True
                        )
                        dv[t] = dv[t] + pf_buf[i * tile_count + t, h : h + 1, :] * ups[i % 2]
            for t in range(tile_count):
                dqkvt_buf[head_rows(2, h), tile(t)] = dv[t].astype(BF16)
        yield
        for i in range(frames):
            spots = [i * tile_count + t for t in range(lane_tiles(i))]
            along = pf_buf[spots[0]] * ds_buf[spots[0]]
            for spot in spots[1:]:
                along = along + pf_buf[spot] * ds_buf[spot]
            along = along + other_half(along)
            for spot in spots:
                ds_buf[spot] = pf_buf[spot] * (ds_buf[spot] - along) * scale
        yield
        for h in range(HEADS):
            keys = [qkvt_buf[head_rows(1, h), tile(t)] for t in range(tile_count)]
            dk = [0.0] * tile_count
            for pair_index in range(tile_count):
                queries = both_frames(qkvt_buf, head_rows(0, h), pair_index)
                dq = []
                for i in (2 * pair_index, 2 * pair_index + 1):
                    part = 0.0
                    for t in range(lane_tiles(i)):
                        ds = ds_buf[i * tile_count + t, h : h + 1, :]
                        part = part + ds * keys[t]
                        dk[t] = dk[t] + ds * queries[i % 2]
                    dq.append(part + other_half(part))
                both = jnp.where(low_frame, dq[0], dq[1])
                dqkvt_buf[head_rows(0, h), tile(pair_index)] = both.astype(BF16)
            for t in range(tile_count):
                dqkvt_buf[head_rows(1, h), tile(t)] = dk[t].astype(BF16)
        yield
        for n in range(3):
            dqkv_buf[:, n * width : (n + 1) * width] = dqkvt_buf[n * width : (n + 1) * width, :].T

    def live_of(chunk):
        cols = cols_ref[lax.div(chunk, WCAP), 0]
        return jnp.where(lax.rem(chunk, WCAP) < cols, 1.0, 0.0).astype(F32)

    def standardize(values):
        centered = values - jnp.mean(values, axis=-1, keepdims=True)
        rstd = lax.rsqrt(jnp.mean(centered * centered, axis=-1, keepdims=True) + EPSILON)
        return centered * rstd, rstd

    blocks = [
        (slice(r, r + ROWS_AT_ONCE), r // window, slice(r % window, r % window + ROWS_AT_ONCE))
        for r in range(0, rows, ROWS_AT_ONCE)
    ]
    ff_parts = [slice(c, c + FF_BLOCK) for c in range(0, hidden, FF_BLOCK)]

    def halves(cols, start=0, step=COLS_AT_ONCE):
        return [slice(c, c + step) for c in range(start, start + cols, step)]

    def forward(spatial, chunk, kept, slot, y_slot):
        kept.x[...] = xbuf[slot]
        for at, f, within in blocks:
            unit, _ = standardize(kept.x[f, within].astype(F32))
            a1_buf[at, :] = (unit * attention_gain[...] + attention_bias[...]).astype(BF16)
        yield
        kept.a1t[...] = a1_buf[...].T
        for part in halves(3 * width, step=width):
            kept.qkv[:, part] = mm(a1_buf[...], projection_in[:, part]).astype(BF16)
        yield
        if spatial:
            yield from window_forward(kept)
            yield
            kept.ot[...] = o_buf[...].T
        else:
            yield from frame_forward(chunk, kept)
            yield
            o_buf[...] = kept.ot[...].T
        wide[...] = mm(o_buf[...], projection_out[...])
        yield
        for at, f, within in blocks:
            middle = kept.x[f, within].astype(F32) + (wide[at, :] + output_bias[...])
            wide[at, :] = middle + down_bias[...]
            unit, rstd = standardize(middle)
            kept.xh2[at, :] = unit.astype(BF16)
            kept.rs2[at, :] = jnp.broadcast_to(rstd, (ROWS_AT_ONCE, 128))
            a2_buf[at, :] = (unit * feedforward_gain[...] + feedforward_bias[...]).astype(BF16)
        yield
        kept.a2t[...] = a2_buf[...].T
        u_buf[0] = mm(a2_buf[...], up_weight[:, ff_parts[0]])
        yield
        for n, part in enumerate(ff_parts):
            if n + 1 < len(ff_parts):
                u_buf[(n + 1) % 2] = mm(a2_buf[...], up_weight[:, ff_parts[n + 1]])
            for at, _, _ in blocks:
                for inner, outer in zip(halves(FF_BLOCK), halves(FF_BLOCK, part.start)):
                    h, slope = gelu_and_slope(u_buf[n % 2, at, inner] + up_bias[:, outer])
                    kept.h[at, outer] = h.astype(BF16)
                    kept.g[at, outer] = slope.astype(BF16)
            yield
        total[...] = mm(kept.h[...], down_weight[...])
        yield
        live = live_of(chunk)
        for at, f, within in blocks:
            ybuf[y_slot, f, within] = ((wide[at, :] + total[at, :]) * live).astype(BF16)
        y_store(chunk).start()
        if spatial:
            y_remote(chunk).start()

    def norm_backward(d_normed, unit, rstd, gain):
        d_unit = d_normed * gain
        along = jnp.mean(d_unit * unit, axis=-1, keepdims=True)
        return rstd * (d_unit - jnp.mean(d_unit, axis=-1, keepdims=True) - unit * along)

    def weight_gradient(total_ref, left, right, cols):
        for part in cols:
            total_ref[:, part] += mm(left[...], right[:, part])

    def backward(spatial, chunk, kept, slot, dx_slot):
        if spatial:
            dx_remote(chunk).wait_recv()
        else:
            dy_load(chunk).wait()

        @pl.when(chunk >= 2)
        def _():
            dx_store(chunk - 2).wait()
            if not spatial:
                dx_remote(chunk - 2).wait_send()

        live = live_of(chunk)
        e_buf[...] = (dybuf[slot].reshape(rows, width).astype(F32) * live).astype(BF16)
        for at, f, within in blocks:
            sum_db[...] += fold8(e_buf[at, :].astype(F32))
        yield
        et_buf[...] = e_buf[...].T
        u_buf[0] = mm_bt(e_buf[...], down_weight[ff_parts[0], :])
        yield
        for n, part in enumerate(ff_parts):
            if n + 1 < len(ff_parts):
                u_buf[(n + 1) % 2] = mm_bt(e_buf[...], down_weight[ff_parts[n + 1], :])
            weight_gradient(d_down_weight, et_buf, kept.h, halves(FF_BLOCK, part.start))
            for at, _, _ in blocks:
                for inner, outer in zip(halves(FF_BLOCK), halves(FF_BLOCK, part.start)):
                    du = u_buf[n % 2, at, inner] * kept.g[at, outer].astype(F32)
                    sum_ub[:, outer] += fold8(du)
                    kept.g[at, outer] = du.astype(BF16)
            yield
        total[...] = mm_bt(kept.g[...], up_weight[...])
        yield
        for n, (at, _, _) in enumerate(blocks):
            if n % 3 == 0:
                weight_gradient(d_up_weight, kept.a2t, kept.g, halves(FF_BLOCK, n // 3 * FF_BLOCK))
            d_normed = total[at, :]
            unit = kept.xh2[at, :].astype(F32)
            sum_fg[...] += fold8(d_normed * unit)
            sum_fb[...] += fold8(d_normed)
            rstd = kept.rs2[at, 0:1]
            d_middle = e_buf[at, :].astype(F32) + norm_backward(d_normed, unit, rstd, feedforward_gain[...])
            wide[at, :] = d_middle
            sum_ob[...] += fold8(d_middle)
            c_buf[at, :] = d_middle.astype(BF16)
        yield
        if spatial:
            do_buf[...] = mm_bt(c_buf[...], projection_out[...]).astype(BF16)
        else:
            dot_buf[...] = mm_bt(projection_out[...], c_buf[...])
        weight_gradient(d_projection_out, kept.ot, c_buf, halves(width))
        yield
        yield from (window_backward(kept) if spatial else frame_backward(kept))
        yield
        total[...] = mm_bt(dqkv_buf[...], projection_in[...])
        yield
        for n, (at, f, within) in enumerate(blocks):
            if n % 2 == 0:
                weight_gradient(d_projection_in, kept.a1t, dqkv_buf, halves(COLS_AT_ONCE, n // 2 * COLS_AT_ONCE))
            d_normed = total[at, :]
            unit, rstd = standardize(kept.x[f, within].astype(F32))
            sum_ag[...] += fold8(d_normed * unit)
            sum_ab[...] += fold8(d_normed)
            dx = wide[at, :] + norm_backward(d_normed, unit, rstd, attention_gain[...])
            do_buf[at, :] = dx.astype(BF16)
        yield
        dxbuf[dx_slot] = do_buf[...].reshape(frames, window, width)
        dx_store(chunk).start()
        if not spatial:
            dx_remote(chunk).start()

    stages = []

    def emit(now, pieces):
        more = True
        while more:
            stages.append(None)

            @pl.when(now + len(stages) > 0)
            def _():
                nonlocal more
                more = next(pieces, "end") is None

    def step(t, carry):
        chunk = t - lead
        ahead = (t, kept_a, lax.rem(t, SLOTS), lax.rem(t, 2))
        behind = (chunk, lax.rem(chunk + SLOTS, SLOTS), lax.rem(chunk + 2, 2))

        @pl.when(t < count)
        def _():
            @pl.when(leading)
            def _():
                x_load(t).wait()

                @pl.when(t + 1 < count)
                def _():
                    x_load(t + 1).start()

            @pl.when(trailing)
            def _():
                y_remote(t).wait_recv()

                @pl.when(t + 1 < count)
                def _():
                    dy_load(t + 1).start()

            @pl.when(t >= 2)
            def _():
                y_store(t - 2).wait()

                @pl.when(leading)
                def _():
                    y_remote(t - 2).wait_send()

        @pl.when(leading & (t > 0) & (t <= count))
        def _():
            wait_all(park(t - 1))

        @pl.when(leading & (t == 1))
        def _():
            start_all(fetch(0))

        @pl.when(leading & (t < count))
        def _():
            emit(t, forward(True, *ahead))
            start_all(park(t))

        @pl.when(leading & (chunk >= 0))
        def _():
            wait_all(fetch(chunk))
            emit(t, backward(True, chunk, kept_b, *behind[1:]))

            @pl.when(chunk + 1 < count)
            def _():
                start_all(fetch(chunk + 1))

        @pl.when(trailing & (t < count))
        def _():
            emit(t, forward(False, *ahead))
            emit(t, backward(False, chunk, kept_a, *behind[1:]))

        return carry

    lax.fori_loop(0, count + LEAD, step, 0)

    vector[0] = jnp.zeros_like(vector[0])
    for row, partial_sum in enumerate((sum_ag, sum_ab, sum_ob, sum_fg, sum_fb, sum_db)):
        vector[0, row : row + 1, :] = jnp.sum(partial_sum[...], axis=0, keepdims=True)
    for n in range(hidden // width):
        up_sum = jnp.sum(sum_ub[:, n * width : (n + 1) * width], axis=0, keepdims=True)
        vector[0, 6 + n : 7 + n, :] = up_sum

    def block_piece(number):
        block, r = divmod(number, width // PIECE)
        at = slice(r * PIECE, (r + 1) * PIECE)
        if block < 3:
            return d_projection_in[at, block * width : (block + 1) * width].astype(BF16)
        if block < 4:
            return d_projection_out[at, :].astype(BF16)
        if block < 8:
            return d_up_weight[at, (block - 4) * width : (block - 3) * width].astype(BF16)
        start = (block - 8) * width + r * PIECE
        return d_down_weight[:, start : start + PIECE].astype(BF16).T

    for number in range(GROUP * UNIT // PIECE):
        u, r = divmod(number, UNIT // PIECE)
        at = slice(r * PIECE, (r + 1) * PIECE)
        packed[u // LINE, at, u % LINE * width : (u % LINE + 1) * width] = block_piece(number)

    for last in (count - 2, count - 1):
        y_store(last).wait()
        dx_store(last).wait()

        @pl.when(leading)
        def _():
            y_remote(last).wait_send()

        @pl.when(trailing)
        def _():
            dx_remote(last).wait_send()

    if not grouped:
        for u in range(GROUP):
            cols = slice(u % LINE * width, (u % LINE + 1) * width)
            pltpu.sync_copy(packed.at[u // LINE, :, cols], flat_ref.at[u * UNIT : (u + 1) * UNIT])
        pltpu.sync_copy(vector.at[0], vector_ref)
        return

    def landing(name, rel, place):
        col = slice(place * width, (place + 1) * width)
        if name == "core":
            return (kept_a.g if rel else kept_a.h).at[:, col]
        if name == "across":
            return kept_b.h.at[ACROSS_FIRST, col]
        if name == "across 2":
            return e_buf.at[:PIECE]
        kind, up = name
        if kind == 1:
            return (kept_b.g if up else kept_a.qkv).at[ACROSS_FIRST, col]
        if up:
            return (kept_b.g if rel else kept_b.h).at[LINE_FIRST, col]
        if rel:
            return dqkv_buf.at[:PIECE, col]
        return kept_a.qkv.at[LINE_FIRST, col]

    sum_over_group(
        packed, result, landing, vector, flat_ref, vector_ref, group_send, group_recv, group_out, ready
    )


def unpack_kernel(flat, vector, d_in, d_out, d_up, d_down, ag, ab, ob, fg, fb, d_up_bias, db):
    block = pl.program_id(0)
    width = flat.shape[1]

    @pl.when(block < 3)
    def _():
        d_in[...] = flat[...].astype(F32)

    @pl.when(block == 3)
    def _():
        d_out[...] = flat[...].astype(F32)

    @pl.when((block > 3) & (block < 8))
    def _():
        d_up[...] = flat[...].astype(F32)

    @pl.when(block > 7)
    def _():
        d_down[...] = flat[...].astype(F32)

    @pl.when(block == 0)
    def _():
        for row, out in enumerate((ag, ab, ob, fg, fb, db)):
            out[...] = vector[row : row + 1, :]
        for n in range(d_up_bias.shape[1] // width):
            d_up_bias[:, n * width : (n + 1) * width] = vector[6 + n : 7 + n, :]


def per_device(
    clip_tokens,
    window_cols,
    time_groups,
    cotangent,
    attention_gain,
    attention_bias,
    projection_in,
    projection_out,
    output_bias,
    feedforward_gain,
    feedforward_bias,
    up_weight,
    up_bias,
    down_weight,
    down_bias,
):
    micro, _, frames, band, width = clip_tokens.shape
    hidden = up_weight.shape[2]
    window = band // WCAP
    rows = frames * window
    weights = (
        attention_gain,
        attention_bias,
        projection_in[0],
        projection_out[0],
        output_bias,
        feedforward_gain,
        feedforward_bias,
        up_weight[0],
        up_bias,
        down_weight[0],
        down_bias,
    )
    smem = pl.BlockSpec(memory_space=pltpu.SMEM)
    vmem = pl.BlockSpec(memory_space=pltpu.VMEM)
    hbm = pl.BlockSpec(memory_space=pl.ANY)
    tokens = jax.ShapeDtypeStruct((micro, frames, band, width), BF16)
    chunk = (frames, window, width)
    group_size = lax.axis_size("dp")
    grouped = group_size % GROUP == 0
    flat_shape = (GROUP * UNIT, width)
    kept_shapes = Kept(
        x=(chunk, BF16),
        a1t=((width, rows), BF16),
        qkv=((rows, 3 * width), BF16),
        p=((rows, width), BF16),
        ot=((width, rows), BF16),
        xh2=((rows, width), BF16),
        a2t=((width, rows), BF16),
        rs2=((rows, 128), F32),
        h=((rows, hidden), BF16),
        g=((rows, hidden), BF16),
    )
    results = pl.pallas_call(
        partial(relay_kernel, (micro, frames, window, width, hidden, grouped)),
        out_shape=(
            tokens,
            tokens,
            jax.ShapeDtypeStruct(flat_shape, BF16),
            jax.ShapeDtypeStruct((VECTOR_ROWS, width), F32),
        )
        + tuple(jax.ShapeDtypeStruct((SLOTS,) + shape, kind) for shape, kind in kept_shapes[1:]),
        in_specs=[smem, smem, hbm, hbm] + [vmem] * len(weights),
        out_specs=[hbm] * (3 + len(kept_shapes)),
        scratch_shapes=[pltpu.VMEM(*kept) for kept in kept_shapes * 2]
        + [
            pltpu.VMEM((width, 3 * width), F32),
            pltpu.VMEM((width, width), F32),
            pltpu.VMEM((width, hidden), F32),
            pltpu.VMEM((width, hidden), F32),
            pltpu.VMEM((SLOTS,) + chunk, BF16),
            pltpu.VMEM((SLOTS,) + chunk, BF16),
            pltpu.VMEM((2,) + chunk, BF16),
            pltpu.VMEM((2,) + chunk, BF16),
            pltpu.VMEM((rows, width), BF16),
            pltpu.VMEM((frames * frames // 2, HEADS, 128), F32),
            pltpu.VMEM((frames * frames // 2, HEADS, 128), F32),
            pltpu.VMEM((rows, width), BF16),
            pltpu.VMEM((rows, width), BF16),
            pltpu.VMEM((rows, width), F32),
            pltpu.VMEM((rows, width), F32),
            pltpu.VMEM((2, rows, FF_BLOCK), F32),
            pltpu.VMEM((rows, width), BF16),
            pltpu.VMEM((width, rows), BF16),
            pltpu.VMEM((rows, width), BF16),
            pltpu.VMEM((rows, width), BF16),
            pltpu.VMEM((rows, 3 * width), BF16),
            pltpu.VMEM((3 * width, rows), F32),
            pltpu.VMEM((width, rows), F32),
            pltpu.VMEM((3 * width, rows), BF16),
            pltpu.VMEM((8, width), F32),
            pltpu.VMEM((8, width), F32),
            pltpu.VMEM((8, width), F32),
            pltpu.VMEM((8, width), F32),
            pltpu.VMEM((8, width), F32),
            pltpu.VMEM((8, hidden), F32),
            pltpu.VMEM((8, width), F32),
            pltpu.SemaphoreType.DMA((SLOTS,)),
            pltpu.SemaphoreType.DMA((SLOTS,)),
            pltpu.SemaphoreType.DMA((2,)),
            pltpu.SemaphoreType.DMA((2,)),
            pltpu.SemaphoreType.DMA((2,)),
            pltpu.SemaphoreType.DMA((2,)),
            pltpu.VMEM((LINE, UNIT, hidden), BF16),
            pltpu.VMEM((LINE, UNIT, hidden), BF16),
            pltpu.SemaphoreType.DMA((len(kept_shapes),)),
            pltpu.SemaphoreType.DMA((len(kept_shapes),)),
            pltpu.VMEM((4 + LINE, VECTOR_ROWS, width), F32),
            pltpu.SemaphoreType.DMA((FAMILIES * LINE,)),
            pltpu.SemaphoreType.DMA((FAMILIES * LINE,)),
            pltpu.SemaphoreType.DMA((2 * GROUP + 1,)),
            pltpu.SemaphoreType.REGULAR((4,)),
        ],
        compiler_params=pltpu.CompilerParams(
            collective_id=0, has_side_effects=True, vmem_limit_bytes=63 * 1024 * 1024
        ),
        name="relay",
    )(
        window_cols,
        time_groups,
        clip_tokens.reshape(micro, frames, band, width),
        cotangent.reshape(micro, frames, band, width),
        *weights,
    )
    activations, input_grads, flat, vector = results[:4]
    if group_size != GROUP:
        groups = None
        if grouped:
            groups = [[first + n for first in range(0, group_size, GROUP)] for n in range(GROUP)]
        flat, vector = lax.psum((flat, vector), "dp", axis_index_groups=groups)
    square = (width, width)
    row = jax.ShapeDtypeStruct((1, width), F32)
    whole_row = pl.BlockSpec((1, width), lambda i: (0, 0))
    wide_row = pl.BlockSpec((1, hidden), lambda i: (0, 0))
    d_in, d_out, d_up, d_down, ag, ab, ob, fg, fb, d_up_bias, db = pl.pallas_call(
        unpack_kernel,
        grid=(GROUP * UNIT // width,),
        in_specs=[
            pl.BlockSpec(square, lambda i: (i, 0)),
            pl.BlockSpec((VECTOR_ROWS, width), lambda i: (0, 0)),
        ],
        out_specs=[
            pl.BlockSpec(square, lambda i: (0, jnp.minimum(i, 2))),
            pl.BlockSpec(square, lambda i: (0, 0)),
            pl.BlockSpec(square, lambda i: (0, jnp.clip(i - 4, 0, 3))),
            pl.BlockSpec(square, lambda i: (jnp.clip(i - 8, 0, 3), 0)),
        ]
        + [whole_row] * 5
        + [wide_row, whole_row],
        out_shape=[
            jax.ShapeDtypeStruct((width, 3 * width), F32),
            jax.ShapeDtypeStruct(square, F32),
            jax.ShapeDtypeStruct((width, hidden), F32),
            jax.ShapeDtypeStruct((hidden, width), F32),
        ]
        + [row] * 5
        + [jax.ShapeDtypeStruct((1, hidden), F32), row],
        name="unpack",
    )(flat, vector)
    shape_out = (1, micro, 1, frames, band, width)
    return (
        activations.reshape(shape_out),
        input_grads.reshape(shape_out),
        ag,
        ab,
        d_in[None],
        d_out[None],
        ob,
        fg,
        fb,
        d_up[None],
        d_up_bias,
        d_down[None],
        db,
    )


def solution(mesh):
    wide, deep = P("section", None), P("section", None, None)
    tokens = P(None, "dp", None, None, None)
    weights = (wide, wide, deep, deep, wide, wide, wide, deep, wide, deep, wide)
    outputs = P("section", None, "dp", None, None, None)
    return jax.shard_map(
        per_device,
        mesh=mesh,
        in_specs=(tokens, P(None, "dp"), P(None, "dp", None), tokens) + weights,
        out_specs=(outputs, outputs) + weights,
        check_vma=False,
    )
```

time: 1640 us -> 329 us (0.20)
  matrix products: 591 us -> 0 us
  local copies, waits for them, and re-layouts: 386 us -> 7.68 us
  waiting for transfers between devices: 342 us -> 0 us
  Pallas kernels: 0 us -> 320 us
  other arithmetic: 132 us -> 0 us
  blocking collectives: 59.4 us -> 0 us
  starting transfers between devices: 58.9 us -> 0 us
  loops' own time: 42.2 us -> 0 us
  between operations: 17.1 us -> 0.65 us
    dot_general x57 -> x0, matrix products: 591 us -> none  [the longest x3 138 us: feedforward_backward(): jnp.einsum('rd,fd->rf', outer_low, down_weight, preferred_element_type=jn...]
    pallas_call x0 -> x2, Pallas kernels: none -> 320 us  [the longest x1 309 us: per_device(): pl.pallas_call(partial(relay_kernel, (micro, frames, window, width, hidde...]
    reshape x33 -> x0, local copies, waits for them, and re-layouts: 179 us -> none  [the longest x3 18.4 us: window_backward(): key_grad.reshape(shape_two)]
    psum x1 -> x0, waiting for transfers between devices: 179 us -> none  [per_device(): lax.psum((attn_gain, attn_bias, attn_in, attn_out, attn_outbias, feed_gai...]
    ppermute x4 -> x0, waiting for transfers between devices: 163 us -> none  [shifted(): lax.ppermute(value, axis, [(source, source + steps) for source in range(i...]
    psum x1 -> x0, blocking collectives: 59.4 us -> none  [per_device(): lax.psum((attn_gain, attn_bias, attn_in, attn_out, attn_outbias, feed_gai...]
    ppermute x4 -> x0, starting transfers between devices: 58.8 us -> none  [shifted(): lax.ppermute(value, axis, [(source, source + steps) for source in range(i...]
    reduce_sum x27 -> x0, other arithmetic: 56.2 us -> none  [the longest x6 15.3 us: normalize(): center = jnp.mean(values, axis=-1, keepdims=True)]
  transfers between devices with their start and end apart: 5 -> 0, of which waited for: 4 -> 0; matrix products, arithmetic and copies ran while one was open for 15% -> 0% of each run, Pallas kernels for 0% -> 0%
where the time goes in v1:
time: 329 us
  Pallas kernels  320 us (97%)
  local copies, waits for them, and re-layouts  7.68 us (2%)
    pallas_call x1, Pallas kernels, per_device(): pl.pallas_call(partial(relay_kernel, (micro, frames, window, width, hidde...  309 us
    pallas_call x1, Pallas kernels, per_device(): pl.pallas_call(unpack_kernel, grid=(GROUP * UNIT // width,), in_specs=[pl...  11.3 us
    unnamed x5, local copies, waits for them, and re-layouts  7.68 us

profile of v1, /device:TPU:1, one launch (start us, length us, event | category | flops | bytes accessed | tf_op | source)
XLA Modules:
  0.0 328.6 jit_solution(5660127126465082934)
XLA Ops:
  0.6 1.3 copy.28.cols_ref
  1.9 308.9 %relay.1 = (bf16[2,6,320,512]{3,2,1,0:T(8,128)(2,1)}, bf16[2,6,320,512]{3,2,1,0:T(8,128)(2,1)}, bf16[6144,512]{1,0:T(8,128)(2,1)}, f32[16,512]{1,0:T(8,128)}, bf...) custom-call(s32[2,1]{1,0:T(2,128)} %copy.28.cols_ref, ...), custom_call_target="tpu_custom_call" | custom-call | tf_op jit(solution)/shard_map/relay/pallas_call | solution.py:1030
  310.9 11.3 %unpack.1 = (f32[512,1536]{1,0:T(8,128)}, f32[512,512]{1,0:T(8,128)}, f32[512,2048]{1,0:T(8,128)}, f32[2048,512]{1,0:T(8,128)}, f32[1,512]{1,0:T(1,128)}, /*inde...) custom-call(bf16[6144,512]{1,0:T(8,128)(2,1)} %get-tuple-element.30., ...), custom_call_target="tpu_custom_call" | custom-call | tf_op jit(solution)/shard_map/unpack/pallas_call | solution.py:1111
  322.2 0.0 copy-start
  322.2 4.5 %copy.33 = bf16[1,2,1,6,320,512]{5,4,3,2,1,0:T(8,128)(2,1)} copy(bf16[1,2,1,6,320,512]{5,4,3,2,1,0:T(8,128)(2,1)} %bitcast.19) | data formatting | bytes 7864320
  326.6 0.0 copy-done
  326.6 1.9 copy.34
Async XLA Ops:
  322.2 4.5 %copy-start = (bf16[2,6,320,512]{3,2,1,0:T(8,128)(2,1)S(1)}, bf16[2,6,320,512]{3,2,1,0:T(8,128)(2,1)}, u32[]{:S(2)}) copy-start(bf16[2,6,320,512]{3,2,1,0:T(8,128)(2,1)} %get-tuple-element.29) | copy-start | bytes 11796484

commit v2 on v1

--- a/solution.py
+++ b/solution.py
@@ -614,9 +614,10 @@
                 both = jnp.where(low_frame, mixed[0], mixed[1])
                 kept.ot[head_rows(0, h), tile(pair_index)] = both.astype(BF16)
 
-    def frame_backward(kept):
+    def frame_backward(kept, beside):
         tile_count = frames // 2
         for h in range(HEADS):
+            beside()
             values = [qkvt_buf[head_rows(2, h), tile(t)] for t in range(tile_count)]
             dv = [0.0] * tile_count
             for pair_index in range(tile_count):
@@ -629,7 +630,6 @@
                         dv[t] = dv[t] + pf_buf[i * tile_count + t, h : h + 1, :] * ups[i % 2]
             for t in range(tile_count):
                 dqkvt_buf[head_rows(2, h), tile(t)] = dv[t].astype(BF16)
-        yield
         for i in range(frames):
             spots = [i * tile_count + t for t in range(lane_tiles(i))]
             along = pf_buf[spots[0]] * ds_buf[spots[0]]
@@ -638,8 +638,8 @@
             along = along + other_half(along)
             for spot in spots:
                 ds_buf[spot] = pf_buf[spot] * (ds_buf[spot] - along) * scale
-        yield
         for h in range(HEADS):
+            beside()
             keys = [qkvt_buf[head_rows(1, h), tile(t)] for t in range(tile_count)]
             dk = [0.0] * tile_count
             for pair_index in range(tile_count):
@@ -656,7 +656,6 @@
                 dqkvt_buf[head_rows(0, h), tile(pair_index)] = both.astype(BF16)
             for t in range(tile_count):
                 dqkvt_buf[head_rows(1, h), tile(t)] = dk[t].astype(BF16)
-        yield
         for n in range(3):
             dqkv_buf[:, n * width : (n + 1) * width] = dqkvt_buf[n * width : (n + 1) * width, :].T
 
@@ -759,7 +758,8 @@
         for n, part in enumerate(ff_parts):
             if n + 1 < len(ff_parts):
                 u_buf[(n + 1) % 2] = mm_bt(e_buf[...], down_weight[ff_parts[n + 1], :])
-            weight_gradient(d_down_weight, et_buf, kept.h, halves(FF_BLOCK, part.start))
+            if spatial:
+                weight_gradient(d_down_weight, et_buf, kept.h, halves(FF_BLOCK, part.start))
             for at, _, _ in blocks:
                 for inner, outer in zip(halves(FF_BLOCK), halves(FF_BLOCK, part.start)):
                     du = u_buf[n % 2, at, inner] * kept.g[at, outer].astype(F32)
@@ -770,7 +770,8 @@
         yield
         for n, (at, _, _) in enumerate(blocks):
             if n % 3 == 0:
-                weight_gradient(d_up_weight, kept.a2t, kept.g, halves(FF_BLOCK, n // 3 * FF_BLOCK))
+                grown = (d_up_weight, kept.a2t, kept.g) if spatial else (d_down_weight, et_buf, kept.h)
+                weight_gradient(*grown, halves(FF_BLOCK, n // 3 * FF_BLOCK))
             d_normed = total[at, :]
             unit = kept.xh2[at, :].astype(F32)
             sum_fg[...] += fold8(d_normed * unit)
@@ -785,10 +786,18 @@
             do_buf[...] = mm_bt(c_buf[...], projection_out[...]).astype(BF16)
         else:
             dot_buf[...] = mm_bt(projection_out[...], c_buf[...])
-        weight_gradient(d_projection_out, kept.ot, c_buf, halves(width))
-        yield
-        yield from (window_backward(kept) if spatial else frame_backward(kept))
-        yield
+        if spatial:
+            weight_gradient(d_projection_out, kept.ot, c_buf, halves(width))
+            yield from window_backward(kept)
+        else:
+            waiting = [(d_up_weight, kept.a2t, kept.g, [part]) for part in halves(hidden)]
+            waiting += [(d_projection_out, kept.ot, c_buf, [part]) for part in halves(width)]
+
+            def beside():
+                if waiting:
+                    weight_gradient(*waiting.pop(0))
+
+            frame_backward(kept, beside)
         total[...] = mm_bt(dqkv_buf[...], projection_in[...])
         yield
         for n, (at, f, within) in enumerate(blocks):
@@ -806,17 +815,9 @@
         if not spatial:
             dx_remote(chunk).start()
 
-    stages = []
-
-    def emit(now, pieces):
-        more = True
-        while more:
-            stages.append(None)
-
-            @pl.when(now + len(stages) > 0)
-            def _():
-                nonlocal more
-                more = next(pieces, "end") is None
+    def emit(pieces):
+        for _ in pieces:
+            pass
 
     def step(t, carry):
         chunk = t - lead
@@ -859,13 +860,13 @@
 
         @pl.when(leading & (t < count))
         def _():
-            emit(t, forward(True, *ahead))
+            emit(forward(True, *ahead))
             start_all(park(t))
 
         @pl.when(leading & (chunk >= 0))
         def _():
             wait_all(fetch(chunk))
-            emit(t, backward(True, chunk, kept_b, *behind[1:]))
+            emit(backward(True, chunk, kept_b, *behind[1:]))
 
             @pl.when(chunk + 1 < count)
             def _():
@@ -873,8 +874,8 @@
 
         @pl.when(trailing & (t < count))
         def _():
-            emit(t, forward(False, *ahead))
-            emit(t, backward(False, chunk, kept_a, *behind[1:]))
+            emit(forward(False, *ahead))
+            emit(backward(False, chunk, kept_a, *behind[1:]))
 
         return carry
 
@@ -945,32 +946,76 @@
     )
 
 
-def unpack_kernel(flat, vector, d_in, d_out, d_up, d_down, ag, ab, ob, fg, fb, d_up_bias, db):
-    block = pl.program_id(0)
-    width = flat.shape[1]
-
-    @pl.when(block < 3)
-    def _():
-        d_in[...] = flat[...].astype(F32)
-
-    @pl.when(block == 3)
-    def _():
-        d_out[...] = flat[...].astype(F32)
-
-    @pl.when((block > 3) & (block < 8))
-    def _():
-        d_up[...] = flat[...].astype(F32)
-
-    @pl.when(block > 7)
-    def _():
-        d_down[...] = flat[...].astype(F32)
-
-    @pl.when(block == 0)
-    def _():
-        for row, out in enumerate((ag, ab, ob, fg, fb, db)):
-            out[...] = vector[row : row + 1, :]
-        for n in range(d_up_bias.shape[1] // width):
-            d_up_bias[:, n * width : (n + 1) * width] = vector[6 + n : 7 + n, :]
+def output_kernel(
+    flat,
+    vector,
+    act,
+    grad,
+    d_in,
+    d_out,
+    d_up,
+    d_down,
+    ag,
+    ab,
+    ob,
+    fg,
+    fb,
+    d_up_bias,
+    db,
+    act_out,
+    grad_out,
+    low,
+    wide,
+    carried,
+    low_sem,
+    wide_sem,
+    in_sem,
+    out_sem,
+):
+    blocks, width, _ = low.shape
+
+    def load(n):
+        return pltpu.make_async_copy(flat.at[n * width : (n + 1) * width], low.at[n], low_sem.at[n])
+
+    def target(n):
+        if n < 3:
+            return d_in.at[:, n * width : (n + 1) * width]
+        if n == 3:
+            return d_out
+        if n < 8:
+            return d_up.at[:, (n - 4) * width : (n - 3) * width]
+        return d_down.at[(n - 8) * width : (n - 7) * width]
+
+    def store(n):
+        return pltpu.make_async_copy(wide.at[n], target(n), wide_sem.at[n])
+
+    arrays = [(ref.at[n], out.at[n]) for ref, out in ((act, act_out), (grad, grad_out)) for n in range(act.shape[0])]
+
+    def bring(n):
+        return pltpu.make_async_copy(arrays[n][0], carried.at[n], in_sem.at[n])
+
+    def take(n):
+        return pltpu.make_async_copy(carried.at[n], arrays[n][1], out_sem.at[n])
+
+    for n in range(blocks):
+        load(n).start()
+    for n in range(len(arrays)):
+        bring(n).start()
+    for row, out in enumerate((ag, ab, ob, fg, fb, db)):
+        out[...] = vector[row : row + 1, :]
+    for n in range(d_up_bias.shape[1] // width):
+        d_up_bias[:, n * width : (n + 1) * width] = vector[6 + n : 7 + n, :]
+    for n in range(blocks):
+        load(n).wait()
+        wide[n] = low[n].astype(F32)
+        store(n).start()
+    for n in range(len(arrays)):
+        bring(n).wait()
+        take(n).start()
+    for n in range(blocks):
+        store(n).wait()
+    for n in range(len(arrays)):
+        take(n).wait()
 
 
 def per_device(
@@ -1106,23 +1151,11 @@
         flat, vector = lax.psum((flat, vector), "dp", axis_index_groups=groups)
     square = (width, width)
     row = jax.ShapeDtypeStruct((1, width), F32)
-    whole_row = pl.BlockSpec((1, width), lambda i: (0, 0))
-    wide_row = pl.BlockSpec((1, hidden), lambda i: (0, 0))
-    d_in, d_out, d_up, d_down, ag, ab, ob, fg, fb, d_up_bias, db = pl.pallas_call(
-        unpack_kernel,
-        grid=(GROUP * UNIT // width,),
-        in_specs=[
-            pl.BlockSpec(square, lambda i: (i, 0)),
-            pl.BlockSpec((VECTOR_ROWS, width), lambda i: (0, 0)),
-        ],
-        out_specs=[
-            pl.BlockSpec(square, lambda i: (0, jnp.minimum(i, 2))),
-            pl.BlockSpec(square, lambda i: (0, 0)),
-            pl.BlockSpec(square, lambda i: (0, jnp.clip(i - 4, 0, 3))),
-            pl.BlockSpec(square, lambda i: (jnp.clip(i - 8, 0, 3), 0)),
-        ]
-        + [whole_row] * 5
-        + [wide_row, whole_row],
+    blocks = GROUP * UNIT // width
+    d_in, d_out, d_up, d_down, ag, ab, ob, fg, fb, d_up_bias, db, activations, input_grads = pl.pallas_call(
+        output_kernel,
+        in_specs=[hbm, vmem, hbm, hbm],
+        out_specs=[hbm] * 4 + [vmem] * 7 + [hbm] * 2,
         out_shape=[
             jax.ShapeDtypeStruct((width, 3 * width), F32),
             jax.ShapeDtypeStruct(square, F32),
@@ -1130,9 +1163,19 @@
             jax.ShapeDtypeStruct((hidden, width), F32),
         ]
         + [row] * 5
-        + [jax.ShapeDtypeStruct((1, hidden), F32), row],
-        name="unpack",
-    )(flat, vector)
+        + [jax.ShapeDtypeStruct((1, hidden), F32), row, tokens, tokens],
+        scratch_shapes=[
+            pltpu.VMEM((blocks,) + square, BF16),
+            pltpu.VMEM((blocks,) + square, F32),
+            pltpu.VMEM((2 * micro, frames, band, width), BF16),
+            pltpu.SemaphoreType.DMA((blocks,)),
+            pltpu.SemaphoreType.DMA((blocks,)),
+            pltpu.SemaphoreType.DMA((2 * micro,)),
+            pltpu.SemaphoreType.DMA((2 * micro,)),
+        ],
+        compiler_params=pltpu.CompilerParams(vmem_limit_bytes=62 * 1024 * 1024),
+        name="outputs",
+    )(flat, vector, activations, input_grads)
     shape_out = (1, micro, 1, frames, band, width)
     return (
         activations.reshape(shape_out),

time: 329 us -> 272 us (0.83)
  Pallas kernels: 320 us -> 269 us
  local copies, waits for them, and re-layouts: 7.68 us -> 1.3 us
    pallas_call x1, Pallas kernels: 309 us -> 256 us  [per_device(): pl.pallas_call(partial(relay_kernel, (micro, frames, window, width, hidde...]
    unnamed x5 -> x1, local copies, waits for them, and re-layouts: 7.68 us -> 1.3 us
where the time goes in v2:
time: 272 us
  Pallas kernels  269 us (99%)
    pallas_call x1, Pallas kernels, per_device(): pl.pallas_call(partial(relay_kernel, (micro, frames, window, width, hidde...  256 us
    pallas_call x1, Pallas kernels, per_device(): pl.pallas_call(output_kernel, in_specs=[hbm, vmem, hbm, hbm], out_specs=[...  13.3 us

profile of v2, /device:TPU:1, one launch (start us, length us, event | category | flops | bytes accessed | tf_op | source)
XLA Modules:
  0.0 271.5 jit_solution(17519368166918340720)
XLA Ops:
  0.6 1.3 copy.28.cols_ref
  1.9 256.2 %relay.1 = (bf16[2,6,320,512]{3,2,1,0:T(8,128)(2,1)}, bf16[2,6,320,512]{3,2,1,0:T(8,128)(2,1)}, bf16[6144,512]{1,0:T(8,128)(2,1)}, f32[16,512]{1,0:T(8,128)}, bf...) custom-call(s32[2,1]{1,0:T(2,128)} %copy.28.cols_ref, ...), custom_call_target="tpu_custom_call" | custom-call | tf_op jit(solution)/shard_map/relay/pallas_call | solution.py:1075
  258.1 13.3 %outputs.1 = (f32[512,1536]{1,0:T(8,128)}, f32[512,512]{1,0:T(8,128)}, f32[512,2048]{1,0:T(8,128)}, f32[2048,512]{1,0:T(8,128)}, f32[1,512]{1,0:T(1,128)}, /*ind...) custom-call(bf16[6144,512]{1,0:T(8,128)(2,1)} %get-tuple-element.30., ...), custom_call_target="tpu_custom_call" | custom-call | tf_op jit(solution)/shard_map/outputs/pallas_call | solution.py:1155

commit v3 on v2

--- a/solution.py
+++ b/solution.py
@@ -337,8 +337,10 @@
 ):
     micro, frames, window, width, hidden, grouped = dims
     parked, scratch = scratch[: len(Kept._fields) - 1], scratch[len(Kept._fields) - 1 :]
-    kept_a, scratch = Kept(*scratch[: len(Kept._fields)]), scratch[len(Kept._fields) :]
-    kept_b, scratch = Kept(*scratch[: len(Kept._fields)]), scratch[len(Kept._fields) :]
+    small = len(Kept._fields) - 2
+    (packed, in_t, out_t, up_t, down_t), scratch = scratch[:5], scratch[5:]
+    kept_a, scratch = Kept(*scratch[:small], packed.at[0], packed.at[1]), scratch[small:]
+    kept_b, scratch = Kept(*scratch[:small], packed.at[2], packed.at[3]), scratch[small:]
     (
     d_projection_in,
     d_projection_out,
@@ -348,11 +350,8 @@
     dybuf,
     ybuf,
     dxbuf,
-    a1_buf,
     pf_buf,
     ds_buf,
-    o_buf,
-    a2_buf,
     wide,
     total,
     u_buf,
@@ -362,7 +361,6 @@
     do_buf,
     dqkv_buf,
     qkvt_buf,
-    dot_buf,
     dqkvt_buf,
     sum_ag,
     sum_ab,
@@ -377,7 +375,6 @@
     y_send,
     dx_sem,
     dx_send,
-    packed,
     result,
     park_sem,
     fetch_sem,
@@ -387,6 +384,7 @@
     group_out,
     ready,
     ) = scratch
+    a1_buf, o_buf, a2_buf, wide_b = do_buf, e_buf, c_buf, wide
     rows = frames * window
     count = micro * WCAP
     head = width // HEADS
@@ -515,13 +513,13 @@
         for at, lanes, n in heads_of:
             keys = of_pair(kept.qkv, at, 1, n)
             total[at, lanes] = mm_bt(keys, by_head(of_pair(kept.qkv, at, 0, n)))
-        yield
+        yield 0
         for at, lanes, n in heads_of:
             scores = total[at, lanes] * scale
             scores = jnp.exp(scores - jnp.max(scores, axis=0, keepdims=True))
             probs = scores * (1.0 / jnp.sum(scores, axis=0, keepdims=True))
             kept.p[at, lanes] = probs.astype(BF16)
-        yield
+        yield 0
         for at, lanes, n in heads_of:
             values = of_pair(kept.qkv, at, 2, n)
             o_buf[at, lanes] = join_heads(mm_at(kept.p[at, lanes], values)).astype(BF16)
@@ -532,13 +530,13 @@
             total[at, lanes] = mm_bt(of_pair(kept.qkv, at, 2, n), up)
             dv = mm(kept.p[at, lanes], up)
             dqkv_buf[at, 2 * width + n * pair : 2 * width + (n + 1) * pair] = dv.astype(BF16)
-        yield
+        yield 0
         for at, lanes, n in heads_of:
             probs = kept.p[at, lanes].astype(F32)
             dp = total[at, lanes]
             ds = probs * (dp - jnp.sum(probs * dp, axis=0, keepdims=True))
             e_buf[at, lanes] = ds.astype(BF16)
-        yield
+        yield 0
         for at, lanes, n in heads_of:
             ds = e_buf[at, lanes]
             dk = mm(ds, by_head(of_pair(kept.qkv, at, 0, n))) * scale
@@ -561,15 +559,17 @@
         return pltpu.roll(values, window, axis=1)
 
     def both_frames(ref, at, t):
-        values = ref[at, tile(t)]
+        values = ref[at, tile(t)].astype(F32)
         turned = other_half(values)
         return jnp.where(low_frame, values, turned), jnp.where(low_frame, turned, values)
 
+    tile_count = frames // 2
+
     def frame_forward(chunk, kept):
-        tile_count = frames // 2
         for n in range(3):
             flat = kept.qkv[:, n * width : (n + 1) * width].T
             qkvt_buf[n * width : (n + 1) * width, :] = flat.astype(F32)
+            yield 150
         for h in range(HEADS):
             keys = [qkvt_buf[head_rows(1, h), tile(t)] for t in range(tile_count)]
             for pair_index in range(tile_count):
@@ -578,7 +578,7 @@
                     for t in range(lane_tiles(i)):
                         score = jnp.sum(queries[i % 2] * keys[t], axis=0, keepdims=True)
                         ds_buf[i * tile_count + t, h : h + 1, :] = score
-        yield
+            yield 120
         item = lax.div(chunk, WCAP)
         labels = [
             jnp.where(low_frame, groups_ref[item, 0, 2 * t], groups_ref[item, 0, 2 * t + 1])
@@ -601,7 +601,7 @@
             whole = 1.0 / (whole + other_half(whole))
             for t, part in enumerate(parts):
                 pf_buf[i * tile_count + t] = part * whole
-        yield
+        yield 150
         for h in range(HEADS):
             values = [qkvt_buf[head_rows(2, h), tile(t)] for t in range(tile_count)]
             for pair_index in range(tile_count):
@@ -613,9 +613,9 @@
                     mixed.append(part + other_half(part))
                 both = jnp.where(low_frame, mixed[0], mixed[1])
                 kept.ot[head_rows(0, h), tile(pair_index)] = both.astype(BF16)
-
-    def frame_backward(kept, beside):
-        tile_count = frames // 2
+            yield 120
+
+    def frame_backward(dot_buf, beside):
         for h in range(HEADS):
             beside()
             values = [qkvt_buf[head_rows(2, h), tile(t)] for t in range(tile_count)]
@@ -630,6 +630,7 @@
                         dv[t] = dv[t] + pf_buf[i * tile_count + t, h : h + 1, :] * ups[i % 2]
             for t in range(tile_count):
                 dqkvt_buf[head_rows(2, h), tile(t)] = dv[t].astype(BF16)
+            yield 220
         for i in range(frames):
             spots = [i * tile_count + t for t in range(lane_tiles(i))]
             along = pf_buf[spots[0]] * ds_buf[spots[0]]
@@ -638,10 +639,12 @@
             along = along + other_half(along)
             for spot in spots:
                 ds_buf[spot] = pf_buf[spot] * (ds_buf[spot] - along) * scale
+        yield 100
         for h in range(HEADS):
             beside()
             keys = [qkvt_buf[head_rows(1, h), tile(t)] for t in range(tile_count)]
             dk = [0.0] * tile_count
+            dq_tiles = []
             for pair_index in range(tile_count):
                 queries = both_frames(qkvt_buf, head_rows(0, h), pair_index)
                 dq = []
@@ -652,12 +655,14 @@
                         part = part + ds * keys[t]
                         dk[t] = dk[t] + ds * queries[i % 2]
                     dq.append(part + other_half(part))
-                both = jnp.where(low_frame, dq[0], dq[1])
-                dqkvt_buf[head_rows(0, h), tile(pair_index)] = both.astype(BF16)
+                dq_tiles.append(jnp.where(low_frame, dq[0], dq[1]))
             for t in range(tile_count):
+                dqkvt_buf[head_rows(0, h), tile(t)] = dq_tiles[t].astype(BF16)
                 dqkvt_buf[head_rows(1, h), tile(t)] = dk[t].astype(BF16)
+            yield 240
         for n in range(3):
             dqkv_buf[:, n * width : (n + 1) * width] = dqkvt_buf[n * width : (n + 1) * width, :].T
+            yield 100
 
     def live_of(chunk):
         cols = cols_ref[lax.div(chunk, WCAP), 0]
@@ -682,21 +687,20 @@
         for at, f, within in blocks:
             unit, _ = standardize(kept.x[f, within].astype(F32))
             a1_buf[at, :] = (unit * attention_gain[...] + attention_bias[...]).astype(BF16)
-        yield
+            yield 90
         kept.a1t[...] = a1_buf[...].T
         for part in halves(3 * width, step=width):
             kept.qkv[:, part] = mm(a1_buf[...], projection_in[:, part]).astype(BF16)
-        yield
+            yield 400
         if spatial:
             yield from window_forward(kept)
-            yield
             kept.ot[...] = o_buf[...].T
         else:
             yield from frame_forward(chunk, kept)
-            yield
             o_buf[...] = kept.ot[...].T
         wide[...] = mm(o_buf[...], projection_out[...])
-        yield
+        yield 400
+        yield "half"
         for at, f, within in blocks:
             middle = kept.x[f, within].astype(F32) + (wide[at, :] + output_bias[...])
             wide[at, :] = middle + down_bias[...]
@@ -704,27 +708,30 @@
             kept.xh2[at, :] = unit.astype(BF16)
             kept.rs2[at, :] = jnp.broadcast_to(rstd, (ROWS_AT_ONCE, 128))
             a2_buf[at, :] = (unit * feedforward_gain[...] + feedforward_bias[...]).astype(BF16)
-        yield
+            yield 110
         kept.a2t[...] = a2_buf[...].T
         u_buf[0] = mm(a2_buf[...], up_weight[:, ff_parts[0]])
-        yield
+        yield 400
         for n, part in enumerate(ff_parts):
             if n + 1 < len(ff_parts):
                 u_buf[(n + 1) % 2] = mm(a2_buf[...], up_weight[:, ff_parts[n + 1]])
+                yield 400
             for at, _, _ in blocks:
                 for inner, outer in zip(halves(FF_BLOCK), halves(FF_BLOCK, part.start)):
                     h, slope = gelu_and_slope(u_buf[n % 2, at, inner] + up_bias[:, outer])
                     kept.h[at, outer] = h.astype(BF16)
                     kept.g[at, outer] = slope.astype(BF16)
-            yield
-        total[...] = mm(kept.h[...], down_weight[...])
-        yield
+                    yield 30
+        u_buf[0] = mm(kept.h[...], down_weight[...])
+        yield 1500
         live = live_of(chunk)
         for at, f, within in blocks:
-            ybuf[y_slot, f, within] = ((wide[at, :] + total[at, :]) * live).astype(BF16)
+            ybuf[y_slot, f, within] = ((wide[at, :] + u_buf[0, at, :]) * live).astype(BF16)
+            yield 15
         y_store(chunk).start()
         if spatial:
             y_remote(chunk).start()
+        yield "half"
 
     def norm_backward(d_normed, unit, rstd, gain):
         d_unit = d_normed * gain
@@ -734,6 +741,7 @@
     def weight_gradient(total_ref, left, right, cols):
         for part in cols:
             total_ref[:, part] += mm(left[...], right[:, part])
+            yield 300
 
     def backward(spatial, chunk, kept, slot, dx_slot):
         if spatial:
@@ -751,73 +759,91 @@
         e_buf[...] = (dybuf[slot].reshape(rows, width).astype(F32) * live).astype(BF16)
         for at, f, within in blocks:
             sum_db[...] += fold8(e_buf[at, :].astype(F32))
-        yield
         et_buf[...] = e_buf[...].T
-        u_buf[0] = mm_bt(e_buf[...], down_weight[ff_parts[0], :])
-        yield
+        u_buf[0] = mm(e_buf[...], down_t[:, ff_parts[0]])
+        yield 600
         for n, part in enumerate(ff_parts):
             if n + 1 < len(ff_parts):
-                u_buf[(n + 1) % 2] = mm_bt(e_buf[...], down_weight[ff_parts[n + 1], :])
+                u_buf[(n + 1) % 2] = mm(e_buf[...], down_t[:, ff_parts[n + 1]])
+                yield 400
             if spatial:
-                weight_gradient(d_down_weight, et_buf, kept.h, halves(FF_BLOCK, part.start))
+                yield from weight_gradient(d_down_weight, et_buf, kept.h, halves(FF_BLOCK, part.start))
             for at, _, _ in blocks:
                 for inner, outer in zip(halves(FF_BLOCK), halves(FF_BLOCK, part.start)):
                     du = u_buf[n % 2, at, inner] * kept.g[at, outer].astype(F32)
                     sum_ub[:, outer] += fold8(du)
                     kept.g[at, outer] = du.astype(BF16)
-            yield
-        total[...] = mm_bt(kept.g[...], up_weight[...])
-        yield
+                    yield 12
+        total[...] = mm(kept.g[...], up_t[...])
+        yield 1500
+        grown = (d_up_weight, kept.a2t, kept.g) if spatial else (d_down_weight, et_buf, kept.h)
+        grown = weight_gradient(*grown, halves(hidden))
         for n, (at, _, _) in enumerate(blocks):
-            if n % 3 == 0:
-                grown = (d_up_weight, kept.a2t, kept.g) if spatial else (d_down_weight, et_buf, kept.h)
-                weight_gradient(*grown, halves(FF_BLOCK, n // 3 * FF_BLOCK))
+            if n % 3 < 2:
+                yield next(grown)
             d_normed = total[at, :]
             unit = kept.xh2[at, :].astype(F32)
             sum_fg[...] += fold8(d_normed * unit)
             sum_fb[...] += fold8(d_normed)
             rstd = kept.rs2[at, 0:1]
             d_middle = e_buf[at, :].astype(F32) + norm_backward(d_normed, unit, rstd, feedforward_gain[...])
-            wide[at, :] = d_middle
+            wide_b[at, :] = d_middle
             sum_ob[...] += fold8(d_middle)
             c_buf[at, :] = d_middle.astype(BF16)
-        yield
+            yield 120
+        yield "half"
         if spatial:
-            do_buf[...] = mm_bt(c_buf[...], projection_out[...]).astype(BF16)
+            do_buf[...] = mm(c_buf[...], out_t[...]).astype(BF16)
         else:
-            dot_buf[...] = mm_bt(projection_out[...], c_buf[...])
+            kept_b.a2t[...] = mm_bt(projection_out[...], c_buf[...]).astype(BF16)
+        yield 400
+        out_gradient = weight_gradient(d_projection_out, kept.ot, c_buf, halves(width))
         if spatial:
-            weight_gradient(d_projection_out, kept.ot, c_buf, halves(width))
+            yield from out_gradient
             yield from window_backward(kept)
         else:
-            waiting = [(d_up_weight, kept.a2t, kept.g, [part]) for part in halves(hidden)]
-            waiting += [(d_projection_out, kept.ot, c_buf, [part]) for part in halves(width)]
+            grown = weight_gradient(d_up_weight, kept.a2t, kept.g, halves(hidden))
 
             def beside():
-                if waiting:
-                    weight_gradient(*waiting.pop(0))
-
-            frame_backward(kept, beside)
-        total[...] = mm_bt(dqkv_buf[...], projection_in[...])
-        yield
+                if next(grown, None) is None:
+                    next(out_gradient, None)
+
+            yield from frame_backward(kept_b.a2t, beside)
+        total[...] = mm(dqkv_buf[...], in_t[...])
+        yield 1100
         for n, (at, f, within) in enumerate(blocks):
             if n % 2 == 0:
-                weight_gradient(d_projection_in, kept.a1t, dqkv_buf, halves(COLS_AT_ONCE, n // 2 * COLS_AT_ONCE))
+                part = halves(COLS_AT_ONCE, n // 2 * COLS_AT_ONCE)
+                yield from weight_gradient(d_projection_in, kept.a1t, dqkv_buf, part)
             d_normed = total[at, :]
             unit, rstd = standardize(kept.x[f, within].astype(F32))
             sum_ag[...] += fold8(d_normed * unit)
             sum_ab[...] += fold8(d_normed)
-            dx = wide[at, :] + norm_backward(d_normed, unit, rstd, attention_gain[...])
+            dx = wide_b[at, :] + norm_backward(d_normed, unit, rstd, attention_gain[...])
             do_buf[at, :] = dx.astype(BF16)
-        yield
+            yield 140
         dxbuf[dx_slot] = do_buf[...].reshape(frames, window, width)
         dx_store(chunk).start()
         if not spatial:
             dx_remote(chunk).start()
+        yield "half"
 
     def emit(pieces):
         for _ in pieces:
             pass
+
+    def transpose_weights():
+        for weight, transposed in (
+            (down_weight, down_t),
+            (up_weight, up_t),
+            (projection_out, out_t),
+            (projection_in, in_t),
+        ):
+            transposed[...] = weight[...].T
+
+    @pl.when(trailing)
+    def _():
+        transpose_weights()
 
     def step(t, carry):
         chunk = t - lead
@@ -834,21 +860,10 @@
                 def _():
                     x_load(t + 1).start()
 
-            @pl.when(trailing)
-            def _():
-                y_remote(t).wait_recv()
-
-                @pl.when(t + 1 < count)
-                def _():
-                    dy_load(t + 1).start()
-
-            @pl.when(t >= 2)
+            @pl.when(leading & (t >= 2))
             def _():
                 y_store(t - 2).wait()
-
-                @pl.when(leading)
-                def _():
-                    y_remote(t - 2).wait_send()
+                y_remote(t - 2).wait_send()
 
         @pl.when(leading & (t > 0) & (t <= count))
         def _():
@@ -872,8 +887,22 @@
             def _():
                 start_all(fetch(chunk + 1))
 
+        @pl.when(leading & (t == 0))
+        def _():
+            transpose_weights()
+
         @pl.when(trailing & (t < count))
         def _():
+            y_remote(t).wait_recv()
+
+            @pl.when(t + 1 < count)
+            def _():
+                dy_load(t + 1).start()
+
+            @pl.when(t >= 2)
+            def _():
+                y_store(t - 2).wait()
+
             emit(forward(False, *ahead))
             emit(backward(False, chunk, kept_a, *behind[1:]))
 
@@ -927,19 +956,21 @@
     def landing(name, rel, place):
         col = slice(place * width, (place + 1) * width)
         if name == "core":
-            return (kept_a.g if rel else kept_a.h).at[:, col]
-        if name == "across":
-            return kept_b.h.at[ACROSS_FIRST, col]
+            return up_t.at[place * width : place * width + UNIT] if rel else down_t.at[:UNIT, col]
         if name == "across 2":
             return e_buf.at[:PIECE]
+        spots = [ref.at[:, n * width : (n + 1) * width] for ref in (kept_a.qkv, kept_b.qkv) for n in range(3)]
+        spots += [kept_a.p, kept_a.xh2, kept_b.p, kept_b.xh2]
+        if name == "across":
+            return spots[place].at[ACROSS_FIRST]
         kind, up = name
         if kind == 1:
-            return (kept_b.g if up else kept_a.qkv).at[ACROSS_FIRST, col]
+            return spots[3 + place if up else 7 + place].at[ACROSS_FIRST]
         if up:
-            return (kept_b.g if rel else kept_b.h).at[LINE_FIRST, col]
+            return spots[3 * rel + place - 1].at[LINE_FIRST]
         if rel:
             return dqkv_buf.at[:PIECE, col]
-        return kept_a.qkv.at[LINE_FIRST, col]
+        return spots[6 + place].at[LINE_FIRST]
 
     sum_over_group(
         packed, result, landing, vector, flat_ref, vector_ref, group_send, group_recv, group_out, ready
@@ -1083,7 +1114,14 @@
         + tuple(jax.ShapeDtypeStruct((SLOTS,) + shape, kind) for shape, kind in kept_shapes[1:]),
         in_specs=[smem, smem, hbm, hbm] + [vmem] * len(weights),
         out_specs=[hbm] * (3 + len(kept_shapes)),
-        scratch_shapes=[pltpu.VMEM(*kept) for kept in kept_shapes * 2]
+        scratch_shapes=[
+            pltpu.VMEM((LINE, UNIT, hidden), BF16),
+            pltpu.VMEM((3 * width, width), BF16),
+            pltpu.VMEM((width, width), BF16),
+            pltpu.VMEM((hidden, width), BF16),
+            pltpu.VMEM((width, hidden), BF16),
+        ]
+        + [pltpu.VMEM(*kept) for kept in kept_shapes[:-2] * 2]
         + [
             pltpu.VMEM((width, 3 * width), F32),
             pltpu.VMEM((width, width), F32),
@@ -1093,11 +1131,8 @@
             pltpu.VMEM((SLOTS,) + chunk, BF16),
             pltpu.VMEM((2,) + chunk, BF16),
             pltpu.VMEM((2,) + chunk, BF16),
-            pltpu.VMEM((rows, width), BF16),
             pltpu.VMEM((frames * frames // 2, HEADS, 128), F32),
             pltpu.VMEM((frames * frames // 2, HEADS, 128), F32),
-            pltpu.VMEM((rows, width), BF16),
-            pltpu.VMEM((rows, width), BF16),
             pltpu.VMEM((rows, width), F32),
             pltpu.VMEM((rows, width), F32),
             pltpu.VMEM((2, rows, FF_BLOCK), F32),
@@ -1107,7 +1142,6 @@
             pltpu.VMEM((rows, width), BF16),
             pltpu.VMEM((rows, 3 * width), BF16),
             pltpu.VMEM((3 * width, rows), F32),
-            pltpu.VMEM((width, rows), F32),
             pltpu.VMEM((3 * width, rows), BF16),
             pltpu.VMEM((8, width), F32),
             pltpu.VMEM((8, width), F32),
@@ -1122,7 +1156,6 @@
             pltpu.SemaphoreType.DMA((2,)),
             pltpu.SemaphoreType.DMA((2,)),
             pltpu.SemaphoreType.DMA((2,)),
-            pltpu.VMEM((LINE, UNIT, hidden), BF16),
             pltpu.VMEM((LINE, UNIT, hidden), BF16),
             pltpu.SemaphoreType.DMA((len(kept_shapes),)),
             pltpu.SemaphoreType.DMA((len(kept_shapes),)),

time: 272 us -> 275 us (1.011)
  Pallas kernels: 269 us -> 272 us
    pallas_call x1, Pallas kernels: 256 us -> 259 us  [per_device(): pl.pallas_call(partial(relay_kernel, (micro, frames, window, width, hidde...]
where the time goes in v3:
time: 275 us; the launch traced here: 274 us
  Pallas kernels  272 us (99%)
    pallas_call x1, Pallas kernels, per_device(): pl.pallas_call(partial(relay_kernel, (micro, frames, window, width, hidde...  259 us
    pallas_call x1, Pallas kernels, per_device(): pl.pallas_call(output_kernel, in_specs=[hbm, vmem, hbm, hbm], out_specs=[...  13.3 us

profile of v3, /device:TPU:1, one launch (start us, length us, event | category | flops | bytes accessed | tf_op | source)
XLA Modules:
  0.0 274.5 jit_solution(8065429466421625530)
XLA Ops:
  0.6 1.3 copy.28.cols_ref
  1.9 259.1 %relay.1 = (bf16[2,6,320,512]{3,2,1,0:T(8,128)(2,1)}, bf16[2,6,320,512]{3,2,1,0:T(8,128)(2,1)}, bf16[6144,512]{1,0:T(8,128)(2,1)}, f32[16,512]{1,0:T(8,128)}, bf...) custom-call(s32[2,1]{1,0:T(2,128)} %copy.28.cols_ref, ...), custom_call_target="tpu_custom_call" | custom-call | tf_op jit(solution)/shard_map/relay/pallas_call | solution.py:1106
  261.0 13.3 %outputs.1 = (f32[512,1536]{1,0:T(8,128)}, f32[512,512]{1,0:T(8,128)}, f32[512,2048]{1,0:T(8,128)}, f32[2048,512]{1,0:T(8,128)}, f32[1,512]{1,0:T(1,128)}, /*ind...) custom-call(bf16[6144,512]{1,0:T(8,128)(2,1)} %get-tuple-element.30., ...), custom_call_target="tpu_custom_call" | custom-call | tf_op jit(solution)/shard_map/outputs/pallas_call | solution.py:1188

commit v4 on v2

--- a/solution.py
+++ b/solution.py
@@ -73,7 +73,7 @@
     return core, across, line, sibling, beside, {"dp": me + 4}, {"dp": me - 4}
 
 
-def sum_over_group(packed, result, landing, vector, flat_ref, vector_ref, send_sem, recv_sem, out_sem, ready):
+def sum_over_group(pack, packed, result, landing, vector, flat_ref, vector_ref, send_sem, recv_sem, out_sem, ready):
     core, across, line, sibling, beside, above, below = group_place()
     sides = (across, 1 - across)
     families = {}
@@ -131,6 +131,8 @@
             condition,
             partial(pl.semaphore_signal, ready.at[there], inc=1, device_id=device, device_id_type=MESH),
         )
+    for half in range(2):
+        pl.when(core == half)(partial(pack, 1 - half))
     pl.semaphore_wait(ready.at[0], 1)
 
     start("vector core", 0, vector.at[0], vector.at[1], sibling)
@@ -140,6 +142,8 @@
             source = unit(packed, 1 - core, side, place, WHOLE)
             start(("core", side), place, source, landing("core", side, place), sibling)
             sent(("core", side), place, source, sibling)
+    for half in range(2):
+        pl.when(core == half)(partial(pack, half))
     pl.semaphore_wait(ready.at[1], 1)
     pl.when(line > 0)(lambda: pl.semaphore_wait(ready.at[2], 1))
     pl.when(line < LINE - 1)(lambda: pl.semaphore_wait(ready.at[3], 1))
@@ -320,14 +324,14 @@
     cot_ref,
     attention_gain,
     attention_bias,
-    projection_in,
-    projection_out,
+    projection_in_ref,
+    projection_out_ref,
     output_bias,
     feedforward_gain,
     feedforward_bias,
-    up_weight,
+    up_weight_ref,
     up_bias,
-    down_weight,
+    down_weight_ref,
     down_bias,
     act_ref,
     grad_ref,
@@ -379,6 +383,11 @@
     dx_send,
     packed,
     result,
+    projection_in,
+    projection_out,
+    up_weight,
+    down_weight,
+    weight_sem,
     park_sem,
     fetch_sem,
     vector,
@@ -462,6 +471,19 @@
             device_id_type=MESH,
         )
 
+    weight_loads = [
+        pltpu.make_async_copy(source, target, weight_sem.at[n])
+        for n, (source, target) in enumerate(
+            (
+                (projection_in_ref, projection_in),
+                (projection_out_ref, projection_out),
+                (up_weight_ref, up_weight),
+                (down_weight_ref, down_weight),
+            )
+        )
+    ]
+    for load in weight_loads:
+        load.start()
     barrier = pltpu.get_barrier_semaphore()
     greeted = 1
     pl.semaphore_signal(barrier, inc=1, device_id=partner, device_id_type=MESH)
@@ -489,6 +511,8 @@
     for total_ref in (sum_ag, sum_ab, sum_ob, sum_fg, sum_fb, sum_ub, sum_db):
         total_ref[...] = jnp.zeros_like(total_ref)
 
+    for load in weight_loads:
+        load.wait()
     pl.semaphore_wait(barrier, greeted)
 
     def frame_rows(i):
@@ -660,7 +684,7 @@
             dqkv_buf[:, n * width : (n + 1) * width] = dqkvt_buf[n * width : (n + 1) * width, :].T
 
     def live_of(chunk):
-        cols = cols_ref[lax.div(chunk, WCAP), 0]
+        cols = cols_ref[0, lax.div(chunk, WCAP)]
         return jnp.where(lax.rem(chunk, WCAP) < cols, 1.0, 0.0).astype(F32)
 
     def standardize(values):
@@ -900,24 +924,30 @@
         start = (block - 8) * width + r * PIECE
         return d_down_weight[:, start : start + PIECE].astype(BF16).T
 
-    for number in range(GROUP * UNIT // PIECE):
-        u, r = divmod(number, UNIT // PIECE)
-        at = slice(r * PIECE, (r + 1) * PIECE)
-        packed[u // LINE, at, u % LINE * width : (u % LINE + 1) * width] = block_piece(number)
-
-    for last in (count - 2, count - 1):
-        y_store(last).wait()
-        dx_store(last).wait()
-
-        @pl.when(leading)
-        def _():
-            y_remote(last).wait_send()
-
-        @pl.when(trailing)
-        def _():
-            dx_remote(last).wait_send()
+    def pack(half):
+        count_half = GROUP * UNIT // PIECE // 2
+        for number in range(half * count_half, (half + 1) * count_half):
+            u, r = divmod(number, UNIT // PIECE)
+            at = slice(r * PIECE, (r + 1) * PIECE)
+            packed[u // LINE, at, u % LINE * width : (u % LINE + 1) * width] = block_piece(number)
+
+    def finish():
+        for last in (count - 2, count - 1):
+            y_store(last).wait()
+            dx_store(last).wait()
+
+            @pl.when(leading)
+            def _():
+                y_remote(last).wait_send()
+
+            @pl.when(trailing)
+            def _():
+                dx_remote(last).wait_send()
 
     if not grouped:
+        pack(0)
+        pack(1)
+        finish()
         for u in range(GROUP):
             cols = slice(u % LINE * width, (u % LINE + 1) * width)
             pltpu.sync_copy(packed.at[u // LINE, :, cols], flat_ref.at[u * UNIT : (u + 1) * UNIT])
@@ -942,8 +972,9 @@
         return kept_a.qkv.at[LINE_FIRST, col]
 
     sum_over_group(
-        packed, result, landing, vector, flat_ref, vector_ref, group_send, group_recv, group_out, ready
+        pack, packed, result, landing, vector, flat_ref, vector_ref, group_send, group_recv, group_out, ready
     )
+    finish()
 
 
 def output_kernel(
@@ -989,7 +1020,12 @@
     def store(n):
         return pltpu.make_async_copy(wide.at[n], target(n), wide_sem.at[n])
 
-    arrays = [(ref.at[n], out.at[n]) for ref, out in ((act, act_out), (grad, grad_out)) for n in range(act.shape[0])]
+    arrays = [
+        (ref.at[n, f], out.at[n, f])
+        for ref, out in ((act, act_out), (grad, grad_out))
+        for n in range(act.shape[0])
+        for f in range(act.shape[1])
+    ]
 
     def bring(n):
         return pltpu.make_async_copy(arrays[n][0], carried.at[n], in_sem.at[n])
@@ -1081,7 +1117,7 @@
             jax.ShapeDtypeStruct((VECTOR_ROWS, width), F32),
         )
         + tuple(jax.ShapeDtypeStruct((SLOTS,) + shape, kind) for shape, kind in kept_shapes[1:]),
-        in_specs=[smem, smem, hbm, hbm] + [vmem] * len(weights),
+        in_specs=[smem, smem, hbm, hbm] + [vmem if value.shape[0] == 1 else hbm for value in weights],
         out_specs=[hbm] * (3 + len(kept_shapes)),
         scratch_shapes=[pltpu.VMEM(*kept) for kept in kept_shapes * 2]
         + [
@@ -1124,6 +1160,11 @@
             pltpu.SemaphoreType.DMA((2,)),
             pltpu.VMEM((LINE, UNIT, hidden), BF16),
             pltpu.VMEM((LINE, UNIT, hidden), BF16),
+            pltpu.VMEM((width, 3 * width), BF16),
+            pltpu.VMEM((width, width), BF16),
+            pltpu.VMEM((width, hidden), BF16),
+            pltpu.VMEM((hidden, width), BF16),
+            pltpu.SemaphoreType.DMA((4,)),
             pltpu.SemaphoreType.DMA((len(kept_shapes),)),
             pltpu.SemaphoreType.DMA((len(kept_shapes),)),
             pltpu.VMEM((4 + LINE, VECTOR_ROWS, width), F32),
@@ -1137,7 +1178,7 @@
         ),
         name="relay",
     )(
-        window_cols,
+        window_cols.T,
         time_groups,
         clip_tokens.reshape(micro, frames, band, width),
         cotangent.reshape(micro, frames, band, width),
@@ -1167,11 +1208,11 @@
         scratch_shapes=[
             pltpu.VMEM((blocks,) + square, BF16),
             pltpu.VMEM((blocks,) + square, F32),
-            pltpu.VMEM((2 * micro, frames, band, width), BF16),
+            pltpu.VMEM((2 * micro * frames, band, width), BF16),
             pltpu.SemaphoreType.DMA((blocks,)),
             pltpu.SemaphoreType.DMA((blocks,)),
-            pltpu.SemaphoreType.DMA((2 * micro,)),
-            pltpu.SemaphoreType.DMA((2 * micro,)),
+            pltpu.SemaphoreType.DMA((2 * micro * frames,)),
+            pltpu.SemaphoreType.DMA((2 * micro * frames,)),
         ],
         compiler_params=pltpu.CompilerParams(vmem_limit_bytes=62 * 1024 * 1024),
         name="outputs",

time: 272 us -> 276 us (1.015)
  Pallas kernels: 269 us -> 275 us
    pallas_call x1, Pallas kernels: 256 us -> 261 us  [per_device(): pl.pallas_call(partial(relay_kernel, (micro, frames, window, width, hidde...]
where the time goes in v4:
time: 276 us
  Pallas kernels  275 us (100%)
    pallas_call x1, Pallas kernels, per_device(): pl.pallas_call(partial(relay_kernel, (micro, frames, window, width, hidde...  261 us
    pallas_call x1, Pallas kernels, per_device(): pl.pallas_call(output_kernel, in_specs=[hbm, vmem, hbm, hbm], out_specs=[...  13.6 us

profile of v4, /device:TPU:1, one launch (start us, length us, event | category | flops | bytes accessed | tf_op | source)
XLA Modules:
  0.0 275.7 jit_solution(11669323503740004855)
XLA Ops:
  0.7 261.2 %relay.1 = (bf16[2,6,320,512]{3,2,1,0:T(8,128)(2,1)}, bf16[2,6,320,512]{3,2,1,0:T(8,128)(2,1)}, bf16[6144,512]{1,0:T(8,128)(2,1)}, f32[16,512]{1,0:T(8,128)}, bf...) custom-call(s32[1,2]{1,0:T(1,128)} %bitcast.23, ...), custom_call_target="tpu_custom_call" | custom-call | tf_op jit(solution)/shard_map/relay/pallas_call | solution.py:1111
  261.9 13.6 %outputs.1 = (f32[512,1536]{1,0:T(8,128)}, f32[512,512]{1,0:T(8,128)}, f32[512,2048]{1,0:T(8,128)}, f32[2048,512]{1,0:T(8,128)}, f32[1,512]{1,0:T(1,128)}, /*ind...) custom-call(bf16[6144,512]{1,0:T(8,128)(2,1)} %get-tuple-element.30., ...), custom_call_target="tpu_custom_call" | custom-call | tf_op jit(solution)/shard_map/outputs/pallas_call | solution.py:1196

commit v5 on v2

--- a/solution.py
+++ b/solution.py
@@ -660,7 +660,7 @@
             dqkv_buf[:, n * width : (n + 1) * width] = dqkvt_buf[n * width : (n + 1) * width, :].T
 
     def live_of(chunk):
-        cols = cols_ref[lax.div(chunk, WCAP), 0]
+        cols = cols_ref[0, lax.div(chunk, WCAP)]
         return jnp.where(lax.rem(chunk, WCAP) < cols, 1.0, 0.0).astype(F32)
 
     def standardize(values):
@@ -905,19 +905,21 @@
         at = slice(r * PIECE, (r + 1) * PIECE)
         packed[u // LINE, at, u % LINE * width : (u % LINE + 1) * width] = block_piece(number)
 
-    for last in (count - 2, count - 1):
-        y_store(last).wait()
-        dx_store(last).wait()
-
-        @pl.when(leading)
-        def _():
-            y_remote(last).wait_send()
-
-        @pl.when(trailing)
-        def _():
-            dx_remote(last).wait_send()
+    def finish():
+        for last in (count - 2, count - 1):
+            y_store(last).wait()
+            dx_store(last).wait()
+
+            @pl.when(leading)
+            def _():
+                y_remote(last).wait_send()
+
+            @pl.when(trailing)
+            def _():
+                dx_remote(last).wait_send()
 
     if not grouped:
+        finish()
         for u in range(GROUP):
             cols = slice(u % LINE * width, (u % LINE + 1) * width)
             pltpu.sync_copy(packed.at[u // LINE, :, cols], flat_ref.at[u * UNIT : (u + 1) * UNIT])
@@ -944,6 +946,7 @@
     sum_over_group(
         packed, result, landing, vector, flat_ref, vector_ref, group_send, group_recv, group_out, ready
     )
+    finish()
 
 
 def output_kernel(
@@ -1137,7 +1140,7 @@
         ),
         name="relay",
     )(
-        window_cols,
+        window_cols.T,
         time_groups,
         clip_tokens.reshape(micro, frames, band, width),
         cotangent.reshape(micro, frames, band, width),

time: 272 us -> 270 us (level)
  no operation moved by 1% of the time
where the time goes in v5:
time: 270 us
  Pallas kernels  269 us (100%)
    pallas_call x1, Pallas kernels, per_device(): pl.pallas_call(partial(relay_kernel, (micro, frames, window, width, hidde...  256 us
    pallas_call x1, Pallas kernels, per_device(): pl.pallas_call(output_kernel, in_specs=[hbm, vmem, hbm, hbm], out_specs=[...  13.3 us

profile of v5, /device:TPU:1, one launch (start us, length us, event | category | flops | bytes accessed | tf_op | source)
XLA Modules:
  0.0 270.2 jit_solution(9332955763413467457)
XLA Ops:
  0.7 256.2 %relay.1 = (bf16[2,6,320,512]{3,2,1,0:T(8,128)(2,1)}, bf16[2,6,320,512]{3,2,1,0:T(8,128)(2,1)}, bf16[6144,512]{1,0:T(8,128)(2,1)}, f32[16,512]{1,0:T(8,128)}, bf...) custom-call(s32[1,2]{1,0:T(1,128)} %bitcast.23, ...), custom_call_target="tpu_custom_call" | custom-call | tf_op jit(solution)/shard_map/relay/pallas_call | solution.py:1078
  256.8 13.3 %outputs.1 = (f32[512,1536]{1,0:T(8,128)}, f32[512,512]{1,0:T(8,128)}, f32[512,2048]{1,0:T(8,128)}, f32[2048,512]{1,0:T(8,128)}, f32[1,512]{1,0:T(1,128)}, /*ind...) custom-call(bf16[6144,512]{1,0:T(8,128)(2,1)} %get-tuple-element.30., ...), custom_call_target="tpu_custom_call" | custom-call | tf_op jit(solution)/shard_map/outputs/pallas_call | solution.py:1158
